TPU v7x, 256 devices: a whole 4x4x8 slice. The times are simulated.
256 devices in a mesh: section: 2 (over core), mp: 4 (over x), dp: 32 (over z, y).
Axes of the slice: x: 4, y: 4, z: 8, core: 2. Of those that a mesh axis runs over, the one named last changes fastest.
Arguments:
- dec_input: bfloat16 [32, 128, 4096], P('dp', 'mp'), may hold values from -6 to 6
- enc_out: bfloat16 [32, 128, 4096], P('dp', ('section', 'mp')), may hold values from -6 to 6
- dec_segment: int32 [32, 128], P('dp'), may hold values from 0 to 3, never falling along the last dimension, each value on 1 to 64 neighbouring positions
- enc_segment: int32 [32, 128], P('dp'), may hold values from 0 to 3, never falling along the last dimension, each value on 1 to 64 neighbouring positions
- norm_gain: float32 [2, 4096], P('section'), may hold values from 0.25 to 1.75
- w_query: bfloat16 [2, 4096, 2048], P('section', 'dp', 'mp'), may hold values from -0.09375 to 0.09375
- w_key: bfloat16 [2, 4096, 2048], P('section', 'dp', 'mp'), may hold values from -0.09375 to 0.09375
- w_value: bfloat16 [2, 4096, 2048], P('section', 'dp', 'mp'), may hold values from -0.09375 to 0.09375
- w_out: bfloat16 [2, 2048, 4096], P('section', 'mp', 'dp'), may hold values from -0.125 to 0.125
- cotangent: bfloat16 [32, 128, 4096], P('dp', 'mp'), may hold values from -6 to 6
Outputs:
- phase_out: bfloat16 [2, 32, 128, 4096], P('section', 'dp', 'mp')
- stream_grad: bfloat16 [2, 32, 128, 4096], P('section', 'dp', 'mp')
- memory_grad: float32 [32, 128, 4096], P('dp', ('section', 'mp'))
Inputs may be any that keep to these rules, and one draw needn't show every extreme that they name: Each replica's rows of dec_segment never fall and name each of the 4 samples at least once. `enc_segment`: as dec_segment, over the encoder rows.
All inputs are finite; a program needn't handle non-finite values.
Results may differ from a plain program's by a relative error of at most 0.03.
Values may be sent and summed in bfloat16 or wider, within the bound.
A program may use at most 64 MiB of HBM per device.

v0:
```python
import jax
import jax.numpy as jnp
from jax import lax
from jax.sharding import PartitionSpec as P

DK = 256


norm_eps = 1e-06


def passed_along(value, axis, steps):
    count = lax.axis_size(axis)
    leading, last = (max(0, -steps), min(count, count - steps))
    return lax.ppermute(value, axis, [(source, source + steps) for source in range(leading, last)])


def matmul_f32(left, right):
    return jnp.dot(left, right, preferred_element_type=jnp.float32)


def matmul_right_t(left, right):
    return lax.dot_general(
        left, right, (((1,), (1,)), ((), ())), preferred_element_type=jnp.float32
    )


def inverse_rms(values):
    return lax.rsqrt(jnp.mean(values * values, axis=-1, keepdims=True) + norm_eps)


def body(
    dec_input,
    enc_out,
    dec_segment,
    enc_segment,
    norm_gain,
    w_query,
    w_key,
    w_value,
    w_out,
    cotangent,
):
    section_count = lax.axis_size("section")
    mp_count = lax.axis_size("mp")
    my_section = lax.axis_index("section")
    score_scale = DK ** (-0.5)
    gain_row = norm_gain[0]
    query_weight, key_weight, value_weight = (
        lax.all_gather(w_query[0], "dp", axis=0, tiled=True),
        lax.all_gather(w_key[0], "dp", axis=0, tiled=True),
        lax.all_gather(w_value[0], "dp", axis=0, tiled=True),
    )
    output_weight = lax.all_gather(w_out[0], "dp", axis=1, tiled=True)
    columns = query_weight.shape[1]
    head_count = columns // DK
    enc_rows = enc_segment.shape[1]
    memory = lax.all_gather(enc_out[0], ("section", "mp"), axis=0, tiled=True)
    keys = matmul_f32(memory, key_weight).astype(jnp.bfloat16)
    values = matmul_f32(memory, value_weight).astype(jnp.bfloat16)
    key_heads = keys.reshape(enc_rows, head_count, DK)
    value_heads = values.reshape(enc_rows, head_count, DK)
    micro_count = 1
    own_input = dec_input[0]
    own_cotangent = cotangent[0]
    own_rows = own_input.shape[0]
    model_width = own_input.shape[1]
    part_rows = own_rows // micro_count
    step_rows = part_rows * mp_count
    step_count = micro_count + section_count - 1
    segment_table = dec_segment[0].reshape(mp_count, micro_count, part_rows)
    enc_ids = enc_segment[0]
    saved_input = jnp.zeros((micro_count, part_rows, model_width), jnp.bfloat16)
    saved_query = jnp.zeros((micro_count, step_rows, columns), jnp.bfloat16)
    saved_prob = jnp.zeros((micro_count, head_count, step_rows, enc_rows), jnp.float32)
    phase_result = jnp.zeros_like(own_input)
    arriving = jnp.zeros((part_rows, model_width), jnp.bfloat16)
    for step_now in range(step_count):
        micro_index = step_now - my_section
        is_live = (micro_index >= 0) & (micro_index < micro_count)
        micro_safe = jnp.clip(micro_index, 0, micro_count - 1)
        if step_now < micro_count:
            fresh_rows = own_input
        else:
            fresh_rows = jnp.zeros((part_rows, model_width), jnp.bfloat16)
        stream = jnp.where(my_section == 0, fresh_rows, arriving)
        widened = stream.astype(jnp.float32)
        hidden = (widened * inverse_rms(widened) * gain_row).astype(jnp.bfloat16)
        query = (
            matmul_f32(lax.all_gather(hidden, "mp", axis=0, tiled=True), query_weight) * score_scale
        ).astype(jnp.bfloat16)
        query_heads = query.reshape(step_rows, head_count, DK)
        scores = jnp.einsum(
            "rhk,ehk->hre", query_heads, key_heads, preferred_element_type=jnp.float32
        )
        row_ids = segment_table.reshape(step_rows)
        scores = jnp.where((row_ids[:, None] == enc_ids[None, :])[None], scores, -1e30)
        row_max = jnp.max(scores, axis=-1, keepdims=True)
        weights = jnp.exp(scores - row_max)
        prob = weights / jnp.sum(weights, axis=-1, keepdims=True)
        attended = (
            jnp.einsum(
                "hre,ehk->rhk",
                prob.astype(jnp.bfloat16),
                value_heads,
                preferred_element_type=jnp.float32,
            )
            .astype(jnp.bfloat16)
            .reshape(step_rows, columns)
        )

        def output_rows(start, count, attended=attended):
            return matmul_f32(attended, output_weight)

        update = lax.psum_scatter(
            output_rows(jnp.int32(0), part_rows * lax.axis_size("mp")).astype(jnp.bfloat16),
            "mp",
            scatter_dimension=0,
            tiled=True,
        ).astype(jnp.float32)
        result = (widened + update).astype(jnp.bfloat16)
        saved_input = jnp.where(
            is_live,
            lax.dynamic_update_index_in_dim(saved_input, stream, micro_safe, 0),
            saved_input,
        )
        saved_query = jnp.where(
            is_live, lax.dynamic_update_index_in_dim(saved_query, query, micro_safe, 0), saved_query
        )
        saved_prob = jnp.where(
            is_live, lax.dynamic_update_index_in_dim(saved_prob, prob, micro_safe, 0), saved_prob
        )
        phase_result = jnp.where(is_live, result, phase_result)
        if step_now + 1 < step_count:
            arriving = passed_along(result, "section", 1)
    key_grad = jnp.zeros((enc_rows, columns), jnp.float32)
    value_grad = jnp.zeros((enc_rows, columns), jnp.float32)
    stream_grad = jnp.zeros_like(own_cotangent)
    arriving_grad = jnp.zeros((part_rows, model_width), jnp.bfloat16)
    for step_now in reversed(range(step_count)):
        micro_index = step_now - my_section
        is_live = (micro_index >= 0) & (micro_index < micro_count)
        micro_safe = jnp.clip(micro_index, 0, micro_count - 1)
        last_index = step_now - (section_count - 1)
        if 0 <= last_index < micro_count:
            fresh_grad = own_cotangent
        else:
            fresh_grad = jnp.zeros((part_rows, model_width), jnp.bfloat16)
        grad = jnp.where(my_section == section_count - 1, fresh_grad, arriving_grad)
        input_rows = lax.dynamic_index_in_dim(saved_input, micro_safe, 0, keepdims=False)
        query_rows = lax.dynamic_index_in_dim(saved_query, micro_safe, 0, keepdims=False)
        prob_saved = lax.dynamic_index_in_dim(saved_prob, micro_safe, 0, keepdims=False)
        saved_heads = query_rows.reshape(step_rows, head_count, DK)
        saved_low = prob_saved.astype(jnp.bfloat16)
        widened_saved = input_rows.astype(jnp.float32)
        inverse_saved = inverse_rms(widened_saved)
        attended_grad = matmul_right_t(
            lax.all_gather(grad, "mp", axis=0, tiled=True), output_weight
        ).astype(jnp.bfloat16)
        attended_heads = attended_grad.reshape(step_rows, head_count, DK)
        prob_grad = jnp.einsum(
            "rhk,ehk->hre", attended_heads, value_heads, preferred_element_type=jnp.float32
        )
        value_term = jnp.einsum(
            "hre,rhk->ehk", saved_low, attended_heads, preferred_element_type=jnp.float32
        )
        score_grad = prob_saved * (
            prob_grad - jnp.sum(prob_grad * prob_saved, axis=-1, keepdims=True)
        )
        query_grad = (
            (
                jnp.einsum(
                    "hre,ehk->rhk", score_grad, key_heads, preferred_element_type=jnp.float32
                )
                * score_scale
            )
            .astype(jnp.bfloat16)
            .reshape(step_rows, columns)
        )
        key_term = jnp.einsum(
            "hre,rhk->ehk", score_grad, saved_heads, preferred_element_type=jnp.float32
        )
        key_grad = key_grad + jnp.where(is_live, key_term.reshape(enc_rows, columns), 0.0)
        value_grad = value_grad + jnp.where(is_live, value_term.reshape(enc_rows, columns), 0.0)

        def hidden_rows(start, count, query_grad=query_grad):
            return matmul_right_t(query_grad, query_weight)

        hidden_grad = lax.psum_scatter(
            hidden_rows(jnp.int32(0), part_rows * lax.axis_size("mp")).astype(jnp.bfloat16),
            "mp",
            scatter_dimension=0,
            tiled=True,
        ).astype(jnp.float32)
        weighted = gain_row * hidden_grad
        norm_grad = inverse_saved * weighted - widened_saved * inverse_saved**3 * jnp.mean(
            widened_saved * weighted, axis=-1, keepdims=True
        )
        input_grad = (grad.astype(jnp.float32) + norm_grad).astype(jnp.bfloat16)
        stream_grad = jnp.where(is_live, input_grad, stream_grad)
        if step_now > 0:
            arriving_grad = passed_along(input_grad, "section", -1)
    key_low = key_grad.astype(jnp.bfloat16)
    value_low = value_grad.astype(jnp.bfloat16)
    memory_grad = lax.psum_scatter(
        (matmul_right_t(key_low, key_weight) + matmul_right_t(value_low, value_weight)).astype(
            jnp.bfloat16
        ),
        ("section", "mp"),
        scatter_dimension=0,
        tiled=True,
    ).astype(jnp.float32)
    return (phase_result[None, None], stream_grad[None, None], memory_grad[None])


def solution(mesh):
    in_specs = (
        P("dp", "mp", None),
        P("dp", ("section", "mp"), None),
        P("dp", None),
        P("dp", None),
        P("section", None),
        P("section", "dp", "mp"),
        P("section", "dp", "mp"),
        P("section", "dp", "mp"),
        P("section", "mp", "dp"),
        P("dp", "mp", None),
    )
    out_specs = (
        P("section", "dp", "mp", None),
        P("section", "dp", "mp", None),
        P("dp", ("section", "mp"), None),
    )
    return jax.shard_map(body, mesh=mesh, in_specs=in_specs, out_specs=out_specs, check_vma=False)
```

profile of v0, /device:TPU:1, one launch (start us, length us, event | category | flops | bytes accessed | tf_op | source)
XLA Modules:
  0.0 658.8 jit_solution(11045677221716469455)
XLA Ops:
  7.2 0.7 all-gather.22.cloned.1.call-update
  7.9 0.7 all-gather.28.cloned.1.call-update
  8.9 1.5 fusion.73
  10.5 0.5 all-gather.26.cloned.1.call-update
  11.1 0.5 all-gather.24.cloned.1.call-update
  11.7 0.5 all-gather.30.cloned.1.call-update
  12.3 0.8 broadcast_compare_fusion
  13.0 27.0 %all-gather.22.cloned.1.call-done = bf16[1,128,4096]{2,1,0:T(8,128)(2,1)} async-done(((bf16[1,16,4096]{2,1,0:T(8,128)(2,1)}), bf16[1,128,4096]{2,1,0:T(8,128)(2,1)}) %all-gather.22.cloned.1.call-update) | async-done | bytes 1048592 | tf_op jit(solution)/shard_map/all_gather | solution.py:58
  40.0 81.3 %all-gather.28.cloned.1.call-done = bf16[1,4096,512]{2,1,0:T(8,128)(2,1)} async-done(((bf16[1,128,512]{2,1,0:T(8,128)(2,1)}), bf16[1,4096,512]{2,1,0:T(8,128)(2,1)}) %all-gather.28.cloned.1.call-update) | async-done | bytes 4194320 | tf_op jit(solution)/shard_map/all_gather | solution.py:51
  121.3 3.2 fusion.37
  124.7 24.6 %all-gather.16.cloned.1.call-done = bf16[128,4096]{1,0:T(8,128)(2,1)} async-done(((bf16[32,4096]{1,0:T(8,128)(2,1)}), bf16[128,4096]{1,0:T(8,128)(2,1)}) %all-gather.16.cloned.1.call-update) | async-done | bytes 1048592 | tf_op jit(solution)/shard_map/all_gather | solution.py:90
  149.3 82.9 %all-gather.26.cloned.1.call-done = bf16[1,4096,512]{2,1,0:T(8,128)(2,1)} async-done(((bf16[1,128,512]{2,1,0:T(8,128)(2,1)}), bf16[1,4096,512]{2,1,0:T(8,128)(2,1)}) %all-gather.26.cloned.1.call-update) | async-done | bytes 4194320 | tf_op jit(solution)/shard_map/all_gather | solution.py:50
  232.2 3.2 fusion.51
  235.8 77.9 %all-gather.24.cloned.1.call-done = bf16[1,4096,512]{2,1,0:T(8,128)(2,1)} async-done(((bf16[1,128,512]{2,1,0:T(8,128)(2,1)}), bf16[1,4096,512]{2,1,0:T(8,128)(2,1)}) %all-gather.24.cloned.1.call-update) | async-done | bytes 4194320 | tf_op jit(solution)/shard_map/all_gather | solution.py:52
  313.8 2.9 fusion.34
  317.0 79.0 %all-gather.30.cloned.1.call-done = bf16[1,512,4096]{2,1,0:T(8,128)(2,1)} async-done(((bf16[1,512,128]{2,1,0:T(8,128)(2,1)}), bf16[1,512,4096]{2,1,0:T(8,128)(2,1)}) %all-gather.30.cloned.1.call-update) | async-done | bytes 4194320 | tf_op jit(solution)/shard_map/all_gather | solution.py:54
  396.0 3.9 convolution_convert_fusion.3
  400.0 0.7 broadcast_select_fusion
  400.8 27.3 %reduce-scatter.6.cloned.1.call-done = bf16[32,4096]{1,0:T(8,128)(2,1)} async-done(((bf16[128,4096]{1,0:T(8,128)(2,1)}), bf16[32,4096]{1,0:T(8,128)(2,1)}) %reduce-scatter.6.cloned.1.call-update) | async-done | bytes 262160 | tf_op jit(solution)/shard_map/reduce_scatter | solution.py:115
  428.2 1.0 fusion.74
  429.2 1.3 collective-permute-start
  430.5 3.1 collective-permute-done
  433.8 0.8 fusion.69
  434.7 22.8 %all-gather.32.cloned.1.call-done = bf16[1,128,4096]{2,1,0:T(8,128)(2,1)} async-done(((bf16[1,32,4096]{2,1,0:T(8,128)(2,1)}), bf16[1,128,4096]{2,1,0:T(8,128)(2,1)}) %all-gather.32.cloned.1.call-update) | async-done | bytes 1048592 | tf_op jit(solution)/shard_map/all_gather | solution.py:158
  457.5 4.0 fusion.40
  461.7 25.3 %all-gather.18.cloned.1.call-done = bf16[128,4096]{1,0:T(8,128)(2,1)} async-done(((bf16[32,4096]{1,0:T(8,128)(2,1)}), bf16[128,4096]{1,0:T(8,128)(2,1)}) %all-gather.18.cloned.1.call-update) | async-done | bytes 1048592 | tf_op jit(solution)/shard_map/all_gather | solution.py:90
  486.9 3.4 select_select_fusion
  491.1 2.5 convolution_convert_fusion.1
  493.6 26.1 %reduce-scatter.10.cloned.1.call-done = bf16[32,4096]{1,0:T(8,128)(2,1)} async-done(((bf16[128,4096]{1,0:T(8,128)(2,1)}), bf16[32,4096]{1,0:T(8,128)(2,1)}) %reduce-scatter.10.cloned.1.call-update) | async-done | bytes 262160 | tf_op jit(solution)/shard_map/reduce_scatter | solution.py:189
  519.7 1.3 fusion.75
  521.0 1.2 fusion.63
  522.1 3.9 collective-permute-start.1
  526.1 1.1 collective-permute-done.1
  527.2 0.7 broadcast_select_fusion.1
  528.0 0.2 convolution_convert_fusion.4
  528.2 3.9 convolution_convert_fusion.2
  532.2 20.9 %all-gather.20.cloned.1.call-done = bf16[128,4096]{1,0:T(8,128)(2,1)} async-done(((bf16[32,4096]{1,0:T(8,128)(2,1)}), bf16[128,4096]{1,0:T(8,128)(2,1)}) %all-gather.20.cloned.1.call-update) | async-done | bytes 1048592 | tf_op jit(solution)/shard_map/all_gather | solution.py:158
  553.1 4.0 fusion.43
  557.7 4.7 convolution_convert_fusion
  563.6 4.0 fusion.9
  567.6 2.5 fusion.2
  570.1 11.4 %reduce-scatter.8.cloned.1.call-done = bf16[32,4096]{1,0:T(8,128)(2,1)} async-done(((bf16[128,4096]{1,0:T(8,128)(2,1)}), bf16[32,4096]{1,0:T(8,128)(2,1)}) %reduce-scatter.8.cloned.1.call-update) | async-done | bytes 262160 | tf_op jit(solution)/shard_map/reduce_scatter | solution.py:115
  581.5 1.8 fusion.79
  583.3 26.8 %reduce-scatter.12.cloned.1.call-done = bf16[32,4096]{1,0:T(8,128)(2,1)} async-done(((bf16[128,4096]{1,0:T(8,128)(2,1)}), bf16[32,4096]{1,0:T(8,128)(2,1)}) %reduce-scatter.12.cloned.1.call-update) | async-done | bytes 262160 | tf_op jit(solution)/shard_map/reduce_scatter | solution.py:189
  610.1 1.1 fusion.77
  611.3 1.9 fusion.81
  613.2 37.5 %reduce-scatter.14.cloned.1.call-done = bf16[16,4096]{1,0:T(8,128)(2,1)} async-done(((bf16[128,4096]{1,0:T(8,128)(2,1)}), bf16[16,4096]{1,0:T(8,128)(2,1)}) %reduce-scatter.14.cloned.1.call-update) | async-done | bytes 131088 | tf_op jit(solution)/shard_map/reduce_scatter | solution.py:205
  650.7 1.6 bitcast_convert_fusion
  (58 shorter events, 4.3 us)
Async XLA Ops:
  7.2 32.8 %all-gather.22.cloned.1.call-start = ((), (), s32[]{:S(2)}) async-start(), calls=%async_computation.13 | async-start | bytes 1179648 | tf_op jit(solution)/shard_map/all_gather | solution.py:58
  7.9 113.4 %all-gather.28.cloned.1.call-start = ((), (), s32[]{:S(2)}) async-start(), calls=%async_computation.16 | async-start | bytes 4325376 | tf_op jit(solution)/shard_map/all_gather | solution.py:51
  8.6 140.6 %all-gather.16.cloned.1.call-start = ((), (), s32[]{:S(2)}) async-start(), calls=%async_computation.5 | async-start | bytes 1310720 | tf_op jit(solution)/shard_map/all_gather | solution.py:90
  10.5 221.8 %all-gather.26.cloned.1.call-start = ((), (), s32[]{:S(2)}) async-start(), calls=%async_computation.15 | async-start | bytes 4325376 | tf_op jit(solution)/shard_map/all_gather | solution.py:50
  11.0 302.7 %all-gather.24.cloned.1.call-start = ((), (), s32[]{:S(2)}) async-start(), calls=%async_computation.14 | async-start | bytes 4325376 | tf_op jit(solution)/shard_map/all_gather | solution.py:52
  11.6 384.4 %all-gather.30.cloned.1.call-start = ((), (), s32[]{:S(2)}) async-start(), calls=%async_computation.17 | async-start | bytes 4325376 | tf_op jit(solution)/shard_map/all_gather | solution.py:54
  12.2 416.0 %reduce-scatter.6.cloned.1.call-start = ((), (), s32[]{:S(2)}) async-start(), calls=%async_computation.6 | async-start | bytes 1310720 | tf_op jit(solution)/shard_map/reduce_scatter | solution.py:115
  124.5 189.2 %copy-start.3 = (bf16[1,128,4096]{2,1,0:T(8,128)(2,1)S(1)}, bf16[1,128,4096]{2,1,0:T(8,128)(2,1)}, u32[]{:S(2)}) copy-start(bf16[1,128,4096]{2,1,0:T(8,128)(2,1)} %all-gather.22.cloned.1.call-done) | copy-start | bytes 3145732
  316.7 83.3 %copy-start.4 = (bf16[1,32,4096]{2,1,0:T(8,128)(2,1)S(1)}, bf16[1,32,4096]{2,1,0:T(8,128)(2,1)}, u32[]{:S(2)}) copy-start(bf16[1,32,4096]{2,1,0:T(8,128)(2,1)} %param.19) | copy-start | bytes 786436
  316.7 111.5 %copy-start.2 = (bf16[1,32,4096]{2,1,0:T(8,128)(2,1)S(1)}, bf16[1,32,4096]{2,1,0:T(8,128)(2,1)}, u32[]{:S(2)}) copy-start(bf16[1,32,4096]{2,1,0:T(8,128)(2,1)} %param.10) | copy-start | bytes 786436
  317.0 116.8 %copy-start.5 = (f32[1,4096]{1,0:T(1,128)S(1)}, f32[1,4096]{1,0:T(1,128)}, u32[]{:S(2)}) copy-start(f32[1,4096]{1,0:T(1,128)} %param.14) | copy-start | bytes 49156
  400.0 57.5 %all-gather.32.cloned.1.call-start = ((), (), s32[]{:S(2)}) async-start(), calls=%async_computation.18 | async-start | bytes 1310720 | tf_op jit(solution)/shard_map/all_gather | solution.py:158
  400.8 86.1 %all-gather.18.cloned.1.call-start = ((), (), s32[]{:S(2)}) async-start(), calls=%async_computation.7 | async-start | bytes 1310720 | tf_op jit(solution)/shard_map/all_gather | solution.py:90
  429.2 4.4 collective-permute-start
  434.6 85.1 %reduce-scatter.10.cloned.1.call-start = ((), (), s32[]{:S(2)}) async-start(), calls=%async_computation.9 | async-start | bytes 1310720 | tf_op jit(solution)/shard_map/reduce_scatter | solution.py:189
  486.9 4.1 copy-start
  493.6 59.6 %all-gather.20.cloned.1.call-start = ((), (), s32[]{:S(2)}) async-start(), calls=%async_computation.10 | async-start | bytes 1310720 | tf_op jit(solution)/shard_map/all_gather | solution.py:158
  522.1 5.1 collective-permute-start.1
  527.9 53.6 %reduce-scatter.8.cloned.1.call-start = ((), (), s32[]{:S(2)}) async-start(), calls=%async_computation.8 | async-start | bytes 1310720 | tf_op jit(solution)/shard_map/reduce_scatter | solution.py:115
  532.2 78.0 %reduce-scatter.12.cloned.1.call-start = ((), (), s32[]{:S(2)}) async-start(), calls=%async_computation.11 | async-start | bytes 1310720 | tf_op jit(solution)/shard_map/reduce_scatter | solution.py:189
  562.4 88.2 %reduce-scatter.14.cloned.1.call-start = ((), (), s32[]{:S(2)}) async-start(), calls=%async_computation.12 | async-start | bytes 1179648 | tf_op jit(solution)/shard_map/reduce_scatter | solution.py:205
  563.0 4.6 copy-start.1
Sparse Core Ops, SparseCore 0:
  9.9 30.0 all-gather.21
  42.6 78.6 all-gather.27
  123.7 25.5 all-gather.15
  151.7 80.4 all-gather.25
  234.6 79.0 all-gather.23
  316.1 79.8 all-gather.29
  400.1 28.0 reduce-scatter.5
  430.7 26.7 all-gather.31
  460.0 26.8 all-gather.17
  493.7 25.9 reduce-scatter.9
  528.1 25.0 all-gather.19
  555.5 25.9 reduce-scatter.7
  584.3 25.8 reduce-scatter.11
  612.5 38.1 reduce-scatter.13
where the time goes:
time: 659 us
  waiting for transfers between devices  578 us (88%)
  matrix products  44.8 us (7%)
  other arithmetic  15.2 us (2%)
  between operations  14.2 us (2%)
    all_gather x1, waiting for transfers between devices, body(): lax.all_gather(w_query[0], 'dp', axis=0, tiled=True)  82.9 us
    all_gather x1, waiting for transfers between devices, body(): lax.all_gather(w_key[0], 'dp', axis=0, tiled=True)  81.3 us
    all_gather x1, waiting for transfers between devices, body(): output_weight = lax.all_gather(w_out[0], 'dp', axis=1, tiled=True)  79 us
    all_gather x1, waiting for transfers between devices, body(): lax.all_gather(w_value[0], 'dp', axis=0, tiled=True)  77.9 us
    reduce_scatter x2, waiting for transfers between devices, body(): lax.psum_scatter(hidden_rows(jnp.int32(0), part_rows * lax.axis_size('mp'...  52.9 us
    all_gather x2, waiting for transfers between devices, body(): lax.all_gather(hidden, 'mp', axis=0, tiled=True)  49.8 us
    all_gather x2, waiting for transfers between devices, body(): lax.all_gather(grad, 'mp', axis=0, tiled=True)  43.7 us
    reduce_scatter x2, waiting for transfers between devices, body(): lax.psum_scatter(output_rows(jnp.int32(0), part_rows * lax.axis_size('mp'...  38.8 us
  transfers between devices with their start and end apart: 16, of which 16 were waited for; matrix products, arithmetic and copies ran while one was open for 7% of the time, Pallas kernels for 0%

commit v1 on v0

v1 whole, which is shorter than its diff:
```python
from types import SimpleNamespace

import jax
import jax.numpy as jnp
from jax import lax
from jax.experimental import pallas as pl
from jax.experimental.pallas import tpu as pltpu
from jax.sharding import PartitionSpec as P

MESH = pl.DeviceIdType.MESH
BF = jnp.bfloat16
F32 = jnp.float32

NX, NY, NZ = 4, 4, 8
D = 4096
DK = 256
COLS = 512
HEADS = COLS // DK
ROWS = 32
EROWS = 16
SL = D // NY
N = 128
EPS = 1e-06
SCALE = DK ** (-0.5)
STAT = 1.0 / (D * SCALE)
Q, K, V, O = range(4)


def vm(*shape, dtype=BF):
    return pltpu.VMEM(shape, dtype)


def dma(*shape):
    return pltpu.SemaphoreType.DMA(shape)


BUFFERS = dict(
    wq=vm(NZ, N, COLS),
    wk=vm(NZ, N, COLS),
    wv=vm(NZ, N, COLS),
    wo=vm(NZ, COLS, N),
    esl=vm(NY, EROWS, SL),
    enc=vm(NY, 2, NX, EROWS, SL),
    sl=vm(NY, ROWS, SL),
    a0=vm(NY, NX, ROWS, SL),
    a1=vm(NY, NX, ROWS, SL),
    dsl=vm(NY, ROWS, SL),
    x0=vm(NY, ROWS, SL),
    c0=vm(NY, ROWS, SL),
    x1=vm(NY, ROWS, SL),
    t1=vm(NY, ROWS, SL),
    t2=vm(NY, ROWS, SL),
    inv0s=vm(ROWS, N, dtype=F32),
    inv0=vm(NY, ROWS, N, dtype=F32),
    inv1=vm(NY, ROWS, N, dtype=F32),
    invx=vm(NX, ROWS, N, dtype=F32),
    gain=vm(8, SL, dtype=F32),
    gain_far=vm(8, SL, dtype=F32),
    mask=vm(N, N, dtype=F32),
    prob=vm(HEADS, N, N, dtype=F32),
    sgt=vm(HEADS, N, N),
    pt=vm(HEADS, N, N),
    q=vm(N, COLS),
    k=vm(N, COLS),
    v=vm(N, COLS),
    ag=vm(N, COLS),
    own_q=vm(N, COLS, dtype=F32),
    own_k=vm(N, COLS, dtype=F32),
    own_v=vm(N, COLS, dtype=F32),
    own_ag=vm(N, COLS, dtype=F32),
    s_q=vm(NY, N, COLS),
    s_k=vm(NY, N, COLS),
    s_v=vm(NY, N, COLS),
    s_ag=vm(NY, N, COLS),
    r_q=vm(NY, N, COLS),
    r_k=vm(NY, N, COLS),
    r_v=vm(NY, N, COLS),
    r_ag=vm(NY, N, COLS),
    at=vm(NY, NX, ROWS, COLS),
    qg=vm(NY, NX, ROWS, COLS),
    kg=vm(NY, 2, NX, EROWS, COLS),
    vg=vm(NY, 2, NX, EROWS, COLS),
    sxa=vm(NX, NY, ROWS, SL),
    sxb=vm(NX, NY, ROWS, SL),
    rxa=vm(NX, NY, ROWS, SL),
    rxb=vm(NX, NY, ROWS, SL),
    ss=vm(NY, NY, ROWS, N, dtype=F32),
    sp=vm(NX, ROWS, N, dtype=F32),
    spr1=vm(NX, ROWS, N, dtype=F32),
    spr0=vm(NX, ROWS, N, dtype=F32),
    sall1=vm(NY, ROWS, N, dtype=F32),
    sall0=vm(NY, ROWS, N, dtype=F32),
    por=vm(NY, ROWS, SL),
    sgr=vm(NY, ROWS, SL),
    mgs=vm(NX, NY, EROWS, SL),
    mgk=vm(NX, NY, EROWS, SL, dtype=F32),
    mgc=vm(NX, NY, EROWS, SL),
    rms=vm(NX, NY, EROWS, SL),
    rm=vm(NX, NY, EROWS, SL),
    mos=vm(NY, EROWS, SL),
    mo=vm(NY, EROWS, SL),
)

COPIES = dict(
    ring=(4, 2, 4),
    enc=(NY, NX),
    sl=(NY, NX),
    dsl=(NY,),
    inv0=(NY,),
    gain=(1,),
    ehalf=(1,),
    c0=(1,),
    pq=(NY,),
    pk=(NY,),
    pv=(NY,),
    pag=(NY,),
    at=(NY,),
    qg=(NY,),
    kg=(NY,),
    vg=(NY,),
    xa=(NX,),
    xb=(NX,),
    a1=(NX,),
    ss=(NY,),
    invx=(NX,),
    inv1=(1,),
    x1=(1,),
    spr1=(NX,),
    spr0=(NX,),
    sall1=(NY,),
    sall0=(NY,),
    por=(NY,),
    por1=(NY,),
    sgr=(NY,),
    sgr0=(NY,),
    mgc1=(1,),
    mgc0=(NX,),
    rm=(NX,),
    mo=(NY,),
)


def nn(a, b):
    return jnp.dot(a, b, preferred_element_type=F32)


def nt(a, b):
    return lax.dot_general(a, b, (((1,), (1,)), ((), ())), preferred_element_type=F32)


def kernel(
    dec, enc_in, dseg, eseg, gain_in, wq_in, wk_in, wv_in, wo_in, cot, out_p, out_s, out_m, *scratch
):
    b = SimpleNamespace(**dict(zip(BUFFERS, scratch)))
    rest = scratch[len(BUFFERS) :]
    c = SimpleNamespace(**dict(zip(COPIES, zip(rest[0::2], rest[1::2]))))
    go = rest[-1]

    s = lax.axis_index("section")
    x = lax.axis_index("mp")
    dp = lax.axis_index("dp")
    y = dp % NY
    z = dp // NY
    far = 1 - s

    def dev(sec, xx, yy, zz=None):
        return {"section": sec, "mp": xx, "dp": (z if zz is None else zz) * NY + yy}

    def copy(name, src, dst, si, ri, device):
        return pltpu.make_async_remote_copy(
            src_ref=src,
            dst_ref=dst,
            send_sem=name[0].at[si],
            recv_sem=name[1].at[ri],
            device_id=device,
            device_id_type=MESH,
        )

    here = dev(s, x, y)

    def got(name, dst, ri):
        copy(name, dst, dst, ri, ri, here).wait_recv()

    def sent(name, src, si):
        copy(name, src, src, si, si, here).wait_send()

    def each(lo, hi, body):
        lax.fori_loop(lo, hi, lambda i, c: (body(i), c)[1], 0)

    def y_send(name, src_of, dst, sec, k):
        yp = (y + k) % NY
        copy(name, src_of(yp), dst.at[y], yp, y, dev(sec, x, yp)).start()

    def y_got(name, dst):
        each(1, NY, lambda k: got(name, dst.at[(y + k) % NY], (y + k) % NY))

    def y_sent(name, src_of, lo=1):
        each(lo, NY, lambda k: sent(name, src_of((y + k) % NY), (y + k) % NY))

    def x_got(name, dst, lo=1):
        each(lo, NX, lambda k: got(name, dst((x + k) % NX), (x + k) % NX))

    def x_sent(name, src, lo=1):
        each(lo, NX, lambda k: sent(name, src((x + k) % NX), (x + k) % NX))

    weights = (b.wq, b.wk, b.wv, b.wo)
    weights_in = (wq_in, wk_in, wv_in, wo_in)

    def part(w, slot, step, way):
        ref = weights[w]
        if step < 3:
            return ref.at[slot]
        half = ref.shape[1] // 2
        return ref.at[slot, pl.ds(way * half, half)]

    def ring_send(w, step):
        for way in range(2):
            slot = (z + NZ - step) % NZ if way == 0 else (z + step) % NZ
            to = (z + 1) % NZ if way == 0 else (z + NZ - 1) % NZ
            ref = part(w, slot, step, way)
            copy(c.ring, ref, ref, (w, way, step), (w, way, step), dev(s, x, y, to)).start()

    def ring_got(w, step):
        for way in range(2):
            slot = (z + NZ - 1 - step) % NZ if way == 0 else (z + 1 + step) % NZ
            got(c.ring, part(w, slot, step, way), (w, way, step))

    def ring_sent():
        for w in range(4):
            for step in range(4):
                for way in range(2):
                    slot = (z + NZ - step) % NZ if way == 0 else (z + step) % NZ
                    sent(c.ring, part(w, slot, step, way), (w, way, step))

    def ring_next(w, step):
        ring_got(w, step - 1)
        ring_send(w, step)

    barrier = pltpu.get_barrier_semaphore()

    def hello(device):
        pl.semaphore_signal(barrier, inc=1, device_id=device, device_id_type=MESH)

    def hello_xy(k):
        t = (NX * y + x + k) % (NX * NY)
        hello(dev(s, t % NX, t // NX))

    each(1, NX * NY, hello_xy)
    hello(dev(s, x, y, (z + 1) % NZ))
    hello(dev(s, x, y, (z + NZ - 1) % NZ))
    each(0, NX, lambda k: hello(dev(far, (x + k) % NX, y)))
    each(1, NY, lambda k: hello(dev(far, x, (y + k) % NY)))

    for w in range(4):
        weights[w][z] = weights_in[w][...]

    def pick(value, yp):
        return jnp.concatenate(
            [value[:, (NY * f + yp) * N : (NY * f + yp + 1) * N] for f in range(NZ)], axis=1
        )

    rows_in = dec[...]
    wide = rows_in.astype(F32)
    inverse = lax.rsqrt(jnp.mean(wide * wide, axis=-1, keepdims=True) + EPS)
    inv_tile = jnp.broadcast_to(inverse, (ROWS, N))
    b.inv0s[...] = inv_tile
    b.inv0[y] = inv_tile
    enc_rows = enc_in[...]

    @pl.when(s == 0)
    def _():
        hidden = (wide * inverse * gain_in[...]).astype(BF)
        for yp in range(NY):
            b.sl[yp] = pick(hidden, yp)

    @pl.when(s == 1)
    def _():
        value = cot[...]
        for yp in range(NY):
            b.sl[yp] = pick(value, yp)

    for yp in range(NY):
        b.dsl[yp] = pick(rows_in, yp)
        b.esl[yp] = pick(enc_rows, yp)
    b.a0[y, x] = b.sl[y]
    b.x0[y] = b.dsl[y]
    b.enc[y, s, x] = b.esl[y]
    for f in range(NZ):
        own_gain = gain_in[:, pl.ds(pl.multiple_of((NY * f + y) * N, N), N)]
        b.gain[:, f * N : (f + 1) * N] = jnp.broadcast_to(own_gain, (8, N))
    dec_ids = jnp.broadcast_to(dseg[...].astype(F32), (N, N)).T
    enc_ids = jnp.broadcast_to(eseg[...].astype(F32), (N, N))
    b.mask[...] = jnp.where(dec_ids == enc_ids, 1.0, 0.0)

    pl.semaphore_wait(barrier, NX * NY - 1 + 2 + NX + NY - 1)

    @pl.when(s == 0)
    def _():
        ring_send(Q, 0)
        ring_send(K, 0)

    def xy_start(name, src, dst):
        def one(k):
            t = (NX * y + x + k) % (NX * NY)
            yp, xp = t // NX, t % NX
            copy(name, src.at[yp], dst, (yp, xp), (y, x), dev(s, xp, yp)).start()

        each(1, NX * NY, one)

    def xy_got(name, dst):
        def one(k):
            t = (NX * y + x + k) % (NX * NY)
            got(name, dst(t // NX, t % NX), (t // NX, t % NX))

        each(1, NX * NY, one)

    def xy_sent(name, src):
        def one(k):
            t = (NX * y + x + k) % (NX * NY)
            sent(name, src.at[t // NX], (t // NX, t % NX))

        each(1, NX * NY, one)

    xy_start(c.sl, b.sl, b.a0.at[y, x])
    xy_start(c.enc, b.esl, b.enc.at[y, s, x])
    each(1, NY, lambda k: y_send(c.dsl, lambda i: b.dsl.at[i], b.x0, s, k))
    each(1, NY, lambda k: y_send(c.inv0, lambda i: b.inv0s, b.inv0, s, k))
    copy(c.gain, b.gain, b.gain_far, 0, 0, dev(far, x, y)).start()

    def enc_half():
        xy_got(c.enc, lambda yp, xp: b.enc.at[yp, s, xp])
        copy(c.ehalf, b.enc.at[:, s], b.enc.at[:, s], 0, 0, dev(far, x, y)).start()

    def enc_whole():
        got(c.ehalf, b.enc.at[:, far], 0)

    def times(w, a):
        return nn(a, weights[w][...].reshape(NZ * N, COLS))

    def pair(p):
        return jnp.concatenate([b.wo[2 * p], b.wo[2 * p + 1]], axis=1)

    def times_out_t(a):
        total = nt(a[:, : 2 * N], pair(0))
        for p in range(1, NZ // 2):
            total += nt(a[:, 2 * N * p : 2 * N * (p + 1)], pair(p))
        return total

    def project(name, rows_of, product, stage, landing, own):
        def one(k):
            yp = (y + k) % NY
            stage[yp] = product(rows_of(yp)).astype(BF)
            y_send(name, lambda i: stage.at[i], landing, s, k)

        each(1, NY, one)
        own[...] = product(rows_of(y))

    def projected(name, landing, own):
        y_got(name, landing)
        total = own[...]
        for k in range(1, NY):
            total += landing[(y + k) % NY].astype(F32)
        return total

    def act(buffer):
        return lambda yp: buffer[yp].reshape(N, SL)

    def head(value, h):
        return value[:, h * DK : (h + 1) * DK]

    def probabilities():
        for h in range(HEADS):
            scores = nt(head(b.q, h), head(b.k, h))
            scores = jnp.where(b.mask[...] > 0.5, scores, -1e30)
            top = jnp.max(scores, axis=-1, keepdims=True)
            e = jnp.exp(scores - top)
            b.prob[h] = e / jnp.sum(e, axis=-1, keepdims=True)

    def attend():
        joined = jnp.concatenate(
            [nn(b.prob[h].astype(BF), head(b.v, h)) for h in range(HEADS)], axis=1
        ).astype(BF)
        b.at[y] = joined.reshape(NX, ROWS, COLS)
        each(1, NY, lambda k: y_send(c.at, lambda i: b.at.at[y], b.at, s, k))

    def query_gradient():
        grads = []
        for h in range(HEADS):
            prob = b.prob[h]
            prob_grad = nt(head(b.ag, h), head(b.v, h))
            score_grad = prob * (prob_grad - jnp.sum(prob_grad * prob, axis=-1, keepdims=True))
            b.sgt[h] = score_grad.T.astype(BF)
            b.pt[h] = prob.T.astype(BF)
            grads.append(nn(score_grad.astype(BF), head(b.k, h)) * SCALE)
        low = jnp.concatenate(grads, axis=1).astype(BF)
        b.qg[y] = low.reshape(NX, ROWS, COLS)
        each(1, NY, lambda k: y_send(c.qg, lambda i: b.qg.at[y], b.qg, s, k))
        both = low.astype(F32) * b.q[...].astype(F32)
        lanes = both[:, :N]
        for f in range(1, COLS // N):
            lanes += both[:, f * N : (f + 1) * N]
        b.sp[...] = lanes.reshape(NX, ROWS, N)

    def key_value_gradients():
        key = jnp.concatenate(
            [nn(b.sgt[h], head(b.q, h)) for h in range(HEADS)], axis=1
        ).astype(BF)
        value = jnp.concatenate(
            [nn(b.pt[h], head(b.ag, h)) for h in range(HEADS)], axis=1
        ).astype(BF)
        b.kg[y] = key.reshape(2, NX, EROWS, COLS)
        b.vg[y] = value.reshape(2, NX, EROWS, COLS)
        each(1, NY, lambda k: y_send(c.kg, lambda i: b.kg.at[y], b.kg, s, k))
        each(1, NY, lambda k: y_send(c.vg, lambda i: b.vg.at[y], b.vg, s, k))

    def update_rows(xp, stage):
        a = b.at[:, xp].reshape(N, COLS)
        for p in range(NZ // 2):
            part_out = nn(a, pair(p)).astype(BF).reshape(NY, ROWS, 2 * N)
            stage[xp, :, :, 2 * N * p : 2 * N * (p + 1)] = part_out

    def hidden_rows(xp, stage):
        a = b.qg[:, xp].reshape(N, COLS)
        for p in range(NZ // 2):
            block = b.wq[2 * p : 2 * p + 2].reshape(2 * N, COLS)
            part_out = nt(a, block).astype(BF).reshape(NY, ROWS, 2 * N)
            stage[xp, :, :, 2 * N * p : 2 * N * (p + 1)] = part_out

    def scatter_x(name, rows_into, stage, landing, sec, keep):
        def one(k):
            xp = (x + k) % NX
            rows_into(xp, stage)
            copy(name, stage.at[xp], landing.at[x], xp, x, dev(sec, xp, y)).start()

        if keep:
            each(1, NX, one)
            rows_into(x, stage)
            landing[x] = stage[x]
        else:
            each(1, NX + 1, one)

    def sum_x(landing, yp):
        total = landing[0, yp].astype(F32)
        for i in range(1, NX):
            total += landing[i, yp].astype(F32)
        return total

    def gather_x():
        def one(k):
            xp = (x + k) % NX
            copy(c.a1, b.a1.at[:, x], b.a1.at[:, x], xp, x, dev(s, xp, y)).start()

        each(1, NX, one)

    def across(tile):
        return jnp.concatenate([tile] * (SL // N), axis=1)

    def send_stat(name, landing, keep):
        def one(k):
            xp = (x + k) % NX
            copy(name, b.sp.at[xp], landing.at[x], xp, x, dev(0, xp, y)).start()

        each(1, NX if keep else NX + 1, one)
        if keep:
            landing[x] = b.sp[x]

    def share_stat(name, landing, result, name_out, lo):
        x_got(name, lambda i: landing.at[i], lo)
        lanes = landing[0] + landing[1] + landing[2] + landing[3]
        result[y] = jnp.broadcast_to(jnp.sum(lanes, axis=-1, keepdims=True), (ROWS, N))
        each(1, NY, lambda k: y_send(name_out, lambda i: result.at[y], result, 0, k))

    def norm_gradient(yp, landing, gain_ref, rows, inv_ref, stat_ref, grad):
        u = sum_x(landing, yp) * gain_ref[0:1, :]
        inv = inv_ref[yp]
        coef = inv * inv * stat_ref[yp] * STAT
        wide_rows = rows[yp].astype(F32)
        return (grad[yp].astype(F32) + across(inv) * u - wide_rows * across(coef)).astype(BF)

    def memory_rows(xp):
        key = b.kg[:, :, xp].reshape(N, COLS)
        value = b.vg[:, :, xp].reshape(N, COLS)
        blocks = []
        for p in range(NZ // 2):
            wk_block = b.wk[2 * p : 2 * p + 2].reshape(2 * N, COLS)
            wv_block = b.wv[2 * p : 2 * p + 2].reshape(2 * N, COLS)
            blocks.append((nt(key, wk_block) + nt(value, wv_block)).reshape(NY, 2, EROWS, 2 * N))
        return blocks

    def lanes_of(p):
        return slice(2 * N * p, 2 * N * (p + 1))

    def send_memory(xp):
        copy(c.rm, b.rms.at[xp], b.rm.at[x], xp, x, dev(s, xp, y)).start()

    @pl.when(s == 0)
    def _():
        ring_next(Q, 1)
        ring_next(K, 1)
        enc_half()
        ring_next(Q, 2)
        ring_next(K, 2)
        ring_send(V, 0)
        ring_send(O, 0)
        ring_next(Q, 3)
        ring_next(K, 3)
        xy_got(c.sl, lambda yp, xp: b.a0.at[yp, xp])
        ring_next(V, 1)
        ring_next(O, 1)
        ring_got(Q, 3)
        project(c.pq, act(b.a0), lambda a: times(Q, a), b.s_q, b.r_q, b.own_q)
        ring_next(V, 2)
        ring_next(O, 2)
        enc_whole()
        ring_got(K, 3)
        project(c.pk, act(b.enc), lambda a: times(K, a), b.s_k, b.r_k, b.own_k)
        ring_next(V, 3)
        ring_next(O, 3)
        pl.semaphore_signal(go, inc=1, device_id=dev(1, x, y), device_id_type=MESH)
        b.q[...] = (projected(c.pq, b.r_q, b.own_q) * SCALE).astype(BF)
        ring_got(V, 3)
        project(c.pv, act(b.enc), lambda a: times(V, a), b.s_v, b.r_v, b.own_v)
        b.k[...] = projected(c.pk, b.r_k, b.own_k).astype(BF)
        probabilities()
        b.v[...] = projected(c.pv, b.r_v, b.own_v).astype(BF)
        attend()
        ring_got(O, 3)
        y_got(c.at, b.at)
        scatter_x(c.xa, update_rows, b.sxa, b.rxa, 1, False)

        got(c.gain, b.gain_far, 0)
        got(c.c0, b.c0, 0)
        got(c.x1, b.x1, 0)
        got(c.inv1, b.inv1, 0)
        y_got(c.dsl, b.x0)
        y_got(c.inv0, b.inv0)
        share_stat(c.spr1, b.spr1, b.sall1, c.sall1, 0)
        y_got(c.sall1, b.sall1)
        x_got(c.xa, lambda i: b.rxa.at[i], 0)

        def grad_one(yp):
            g = norm_gradient(
                yp, b.rxa, b.gain_far, b.x1, b.inv1, b.sall1, b.c0
            )
            b.t1[yp] = g
            b.a1[yp, x] = g

        each(0, NY, grad_one)
        gather_x()
        each(1, NY + 1, lambda k: y_send(c.sgr, lambda i: b.t1.at[i], b.sgr, 1, k))

        x_got(c.a1, lambda i: b.a1.at[:, i])
        project(c.pag, act(b.a1), times_out_t, b.s_ag, b.r_ag, b.own_ag)
        b.ag[...] = projected(c.pag, b.r_ag, b.own_ag).astype(BF)
        query_gradient()
        send_stat(c.spr0, b.spr0, True)
        key_value_gradients()
        y_got(c.qg, b.qg)
        scatter_x(c.xb, hidden_rows, b.sxb, b.rxb, 0, True)
        share_stat(c.spr0, b.spr0, b.sall0, c.sall0, 1)
        y_got(c.kg, b.kg)
        y_got(c.vg, b.vg)
        got(c.mgc1, b.mgc, 0)

        def memory_one(k):
            xp = (x + k) % NX
            for p, block in enumerate(memory_rows(xp)):
                b.mgs[xp, :, :, lanes_of(p)] = block[:, 1].astype(BF)
                kept = block[:, 0] + b.mgc[xp, :, :, lanes_of(p)].astype(F32)
                b.rms[xp, :, :, lanes_of(p)] = kept.astype(BF)
            copy(c.mgc0, b.mgs.at[xp], b.mgc.at[xp], xp, xp, dev(1, x, y)).start()

        def memory_send(k):
            memory_one(k)
            send_memory((x + k) % NX)

        each(1, NX, memory_send)
        memory_one(NX)
        b.rm[x] = b.rms[x]

        y_got(c.sall0, b.sall0)
        x_got(c.xb, lambda i: b.rxb.at[i])

        def grad_zero(yp):
            b.t2[yp] = norm_gradient(
                yp, b.rxb, b.gain, b.x0, b.inv0, b.sall0, b.t1
            )

        each(0, NY, grad_zero)
        each(1, NY, lambda k: y_send(c.sgr0, lambda i: b.t2.at[i], b.sgr, 0, k))
        b.sgr[y] = b.t2[y]

    @pl.when(s == 1)
    def _():
        enc_half()
        xy_got(c.sl, lambda yp, xp: b.a0.at[yp, xp])
        copy(c.c0, b.a0.at[:, x], b.c0, 0, 0, dev(0, x, y)).start()
        y_got(c.dsl, b.x0)
        y_got(c.inv0, b.inv0)
        got(c.gain, b.gain_far, 0)
        enc_whole()
        pl.semaphore_wait(go, 1)
        ring_send(K, 0)
        ring_send(V, 0)
        ring_next(K, 1)
        ring_next(V, 1)
        ring_next(K, 2)
        ring_next(V, 2)
        ring_send(O, 0)
        ring_send(Q, 0)
        ring_next(K, 3)
        ring_next(V, 3)
        ring_next(O, 1)
        ring_next(Q, 1)
        ring_got(K, 3)
        project(c.pk, act(b.enc), lambda a: times(K, a), b.s_k, b.r_k, b.own_k)
        ring_next(O, 2)
        ring_next(Q, 2)
        ring_got(V, 3)
        project(c.pv, act(b.enc), lambda a: times(V, a), b.s_v, b.r_v, b.own_v)
        ring_next(O, 3)
        ring_next(Q, 3)
        b.k[...] = projected(c.pk, b.r_k, b.own_k).astype(BF)
        b.v[...] = projected(c.pv, b.r_v, b.own_v).astype(BF)
        ring_got(O, 3)
        project(c.pag, act(b.a0), times_out_t, b.s_ag, b.r_ag, b.own_ag)
        b.ag[...] = projected(c.pag, b.r_ag, b.own_ag).astype(BF)
        ring_got(Q, 3)

        x_got(c.xa, lambda i: b.rxa.at[i], 0)

        def stream_one(yp):
            rows = (b.x0[yp].astype(F32) + sum_x(b.rxa, yp)).astype(BF)
            b.x1[yp] = rows
            rows = rows.astype(F32)
            b.a1[yp, x] = (rows * b.gain[0:1, :]).astype(BF)
            squares = rows * rows
            lanes = squares[:, :N]
            for f in range(1, SL // N):
                lanes += squares[:, f * N : (f + 1) * N]
            b.ss[y, yp] = lanes

        each(0, NY, stream_one)
        gather_x()
        each(1, NY, lambda k: y_send(c.ss, lambda i: b.ss.at[y], b.ss, 1, k))
        copy(c.x1, b.x1, b.x1, 0, 0, dev(0, x, y)).start()
        each(1, NY + 1, lambda k: y_send(c.por, lambda i: b.x1.at[i], b.por, 0, k))
        y_got(c.ss, b.ss)

        def inverse_one(yp):
            lanes = b.ss[0, yp] + b.ss[1, yp] + b.ss[2, yp] + b.ss[3, yp]
            inv = lax.rsqrt(jnp.sum(lanes, axis=-1, keepdims=True) * (1.0 / D) + EPS)
            b.inv1[yp] = jnp.broadcast_to(inv, (ROWS, N))

        each(0, NY, inverse_one)
        b.invx[x] = b.inv1[y]

        def invx_one(k):
            xp = (x + k) % NX
            copy(c.invx, b.inv1.at[y], b.invx.at[x], xp, x, dev(1, xp, y)).start()

        each(1, NX, invx_one)
        copy(c.inv1, b.inv1, b.inv1, 0, 0, dev(0, x, y)).start()
        x_got(c.a1, lambda i: b.a1.at[:, i])
        project(c.pq, act(b.a1), lambda a: times(Q, a), b.s_q, b.r_q, b.own_q)
        x_got(c.invx, lambda i: b.invx.at[i])
        row_scale = b.invx[...].reshape(N, N) * SCALE
        row_scale = jnp.concatenate([row_scale] * (COLS // N), axis=1)
        b.q[...] = (projected(c.pq, b.r_q, b.own_q) * row_scale).astype(BF)
        probabilities()
        query_gradient()
        send_stat(c.spr1, b.spr1, False)
        y_got(c.qg, b.qg)
        scatter_x(c.xa, hidden_rows, b.sxa, b.rxa, 0, False)

        attend()
        key_value_gradients()
        y_got(c.at, b.at)
        scatter_x(c.xb, update_rows, b.sxb, b.rxb, 1, True)
        y_got(c.kg, b.kg)
        y_got(c.vg, b.vg)

        def memory_one(xp):
            for p, block in enumerate(memory_rows(xp)):
                b.mgs[xp, :, :, lanes_of(p)] = block[:, 0].astype(BF)
                b.mgk[xp, :, :, lanes_of(p)] = block[:, 1]

        each(0, NX, memory_one)
        copy(c.mgc1, b.mgs, b.mgc, 0, 0, dev(0, x, y)).start()
        x_got(c.xb, lambda i: b.rxb.at[i])

        def output_one(yp):
            b.t2[yp] = (b.x1[yp].astype(F32) + sum_x(b.rxb, yp)).astype(BF)

        each(0, NY, output_one)
        each(1, NY, lambda k: y_send(c.por1, lambda i: b.t2.at[i], b.por, 1, k))
        b.por[y] = b.t2[y]

        def memory_send(k):
            xp = (x + k) % NX
            got(c.mgc0, b.mgc.at[xp], xp)
            b.rms[xp] = (b.mgk[xp] + b.mgc[xp].astype(F32)).astype(BF)

            @pl.when(k < NX)
            def _():
                send_memory(xp)

        each(1, NX + 1, memory_send)
        b.rm[x] = b.rms[x]

    x_got(c.rm, lambda i: b.rm.at[i])
    total = b.rm[0].astype(F32)
    for i in range(1, NX):
        total += b.rm[i].astype(F32)
    b.mos[...] = total.astype(BF)
    each(1, NY, lambda k: y_send(c.mo, lambda i: b.mos.at[i], b.mo, s, k))
    b.mo[y] = b.mos[y]

    def whole(landing, out):
        for yp in range(NY):
            value = landing[yp]
            for f in range(NZ):
                at = (NY * f + yp) * N
                out[:, at : at + N] = value[:, f * N : (f + 1) * N].astype(out.dtype)

    @pl.when(s == 0)
    def _():
        each(0, NY, lambda i: got(c.por, b.por.at[i], i))
        y_got(c.sgr0, b.sgr)

    @pl.when(s == 1)
    def _():
        y_got(c.por1, b.por)
        each(0, NY, lambda i: got(c.sgr, b.sgr.at[i], i))

    whole(b.por, out_p)
    whole(b.sgr, out_s)
    y_got(c.mo, b.mo)
    whole(b.mo, out_m)

    ring_sent()
    xy_sent(c.sl, b.sl)
    xy_sent(c.enc, b.esl)
    y_sent(c.dsl, lambda i: b.dsl.at[i])
    y_sent(c.inv0, lambda i: b.inv0s)
    sent(c.gain, b.gain, 0)
    sent(c.ehalf, b.enc.at[:, s], 0)
    for name, stage in ((c.pq, b.s_q), (c.pk, b.s_k), (c.pv, b.s_v), (c.pag, b.s_ag)):
        y_sent(name, lambda i, stage=stage: stage.at[i])
    for name, stage in ((c.at, b.at), (c.qg, b.qg), (c.kg, b.kg), (c.vg, b.vg)):
        y_sent(name, lambda i, stage=stage: stage.at[y])
    x_sent(c.rm, lambda i: b.rms.at[i])
    y_sent(c.mo, lambda i: b.mos.at[i])
    x_sent(c.a1, lambda i: b.a1.at[:, x])
    x_sent(c.xa, lambda i: b.sxa.at[i], 0)
    x_sent(c.xb, lambda i: b.sxb.at[i])

    @pl.when(s == 0)
    def _():
        y_sent(c.sgr, lambda i: b.t1.at[i], 0)
        y_sent(c.sgr0, lambda i: b.t2.at[i])
        y_sent(c.sall1, lambda i: b.sall1.at[y])
        y_sent(c.sall0, lambda i: b.sall0.at[y])
        x_sent(c.spr0, lambda i: b.sp.at[i])
        x_sent(c.mgc0, lambda i: b.mgs.at[i], 0)

    @pl.when(s == 1)
    def _():
        sent(c.c0, b.a0.at[:, x], 0)
        y_sent(c.por, lambda i: b.x1.at[i], 0)
        y_sent(c.por1, lambda i: b.t2.at[i])
        sent(c.x1, b.x1, 0)
        sent(c.inv1, b.inv1, 0)
        sent(c.mgc1, b.mgs, 0)
        y_sent(c.ss, lambda i: b.ss.at[y])
        x_sent(c.invx, lambda i: b.inv1.at[y])
        x_sent(c.spr1, lambda i: b.sp.at[i], 0)


def body(*args):
    dec, enc, dseg, eseg, gain, wq, wk, wv, wo, cot = args
    sems = []
    for shape in COPIES.values():
        sems += [dma(*shape), dma(*shape)]
    phase, stream, memory = pl.pallas_call(
        kernel,
        out_shape=(
            jax.ShapeDtypeStruct((ROWS, D), BF),
            jax.ShapeDtypeStruct((ROWS, D), BF),
            jax.ShapeDtypeStruct((EROWS, D), F32),
        ),
        in_specs=[pl.BlockSpec(memory_space=pltpu.VMEM)] * 10,
        out_specs=(pl.BlockSpec(memory_space=pltpu.VMEM),) * 3,
        scratch_shapes=list(BUFFERS.values()) + sems + [pltpu.SemaphoreType.REGULAR],
        compiler_params=pltpu.CompilerParams(
            collective_id=0, has_side_effects=True, vmem_limit_bytes=56 * 2**20
        ),
        cost_estimate=pl.CostEstimate(
            flops=16 * 2**30, bytes_accessed=4 * 2**20, transcendentals=2**16
        ),
        name="decoder_phases",
    )(dec[0], enc[0], dseg, eseg, gain, wq[0], wk[0], wv[0], wo[0], cot[0])
    return phase[None, None], stream[None, None], memory[None]


def solution(mesh):
    in_specs = (
        P("dp", "mp", None),
        P("dp", ("section", "mp"), None),
        P("dp", None),
        P("dp", None),
        P("section", None),
        P("section", "dp", "mp"),
        P("section", "dp", "mp"),
        P("section", "dp", "mp"),
        P("section", "mp", "dp"),
        P("dp", "mp", None),
    )
    out_specs = (
        P("section", "dp", "mp", None),
        P("section", "dp", "mp", None),
        P("dp", ("section", "mp"), None),
    )
    return jax.shard_map(body, mesh=mesh, in_specs=in_specs, out_specs=out_specs, check_vma=False)
```

time: 659 us -> 167 us (0.25)
  waiting for transfers between devices: 578 us -> 0 us
  Pallas kernels: 0 us -> 163 us
  matrix products: 44.8 us -> 0 us
  other arithmetic: 15.2 us -> 0 us
  between operations: 14.2 us -> 0.65 us
    all_gather x9 -> x0, waiting for transfers between devices: 442 us -> none  [the longest x1 82.9 us: body(): lax.all_gather(w_query[0], 'dp', axis=0, tiled=True)]
    pallas_call x0 -> x1, Pallas kernels: none -> 163 us  [body(): pl.pallas_call(kernel, out_shape=(jax.ShapeDtypeStruct((ROWS, D), BF), ja...]
    reduce_scatter x5 -> x0, waiting for transfers between devices: 129 us -> none  [the longest x2 52.9 us: body(): lax.psum_scatter(hidden_rows(jnp.int32(0), part_rows * lax.axis_size('mp'...]
    dot_general x24 -> x0, matrix products: 44.8 us -> none  [the longest x6 21.7 us: matmul_right_t(): lax.dot_general(left, right, (((1,), (1,)), ((), ())), preferred_element_...]
  transfers between devices with their start and end apart: 16 -> 0, of which waited for: 16 -> 0; matrix products, arithmetic and copies ran while one was open for 7% -> 0% of each run, Pallas kernels for 0% -> 0%
where the time goes in v1:
time: 167 us
  Pallas kernels  163 us (98%)
  local copies, waits for them, and re-layouts  3.46 us (2%)
    pallas_call x1, Pallas kernels, body(): pl.pallas_call(kernel, out_shape=(jax.ShapeDtypeStruct((ROWS, D), BF), ja...  163 us
    unnamed x7, local copies, waits for them, and re-layouts  3.46 us

profile of v1, /device:TPU:1, one launch (start us, length us, event | category | flops | bytes accessed | tf_op | source)
XLA Modules:
  0.0 167.2 jit_solution(14764112235778460541)
XLA Ops:
  0.6 163.1 %decoder_phases.1 = (bf16[32,4096]{1,0:T(8,128)(2,1)}, bf16[32,4096]{1,0:T(8,128)(2,1)}, f32[16,4096]{1,0:T(8,128)}) custom-call(bf16[32,4096]{1,0:T(8,128)(2,1)} %bitcast.13, bf16[16,4096]{1,0:T(8,128)(2,1)} %bitcast.15, s32[1,128]{1,0:T(1,128)} %dseg.1, s32[1,128]{1,0:T(1,128)} %eseg.1, f32[1,4096]{1,0:T(1,128)} %gain_in.1, bf16[128,512]{1,0:T(8,128)(2,1)} %bitcast.16, ...), custom_call_target="tpu_custom_call" | custom-call | flops 17179869184 | bytes 4194304 | tf_op jit(solution)/shard_map/decoder_phases/pallas_call | solution.py:785
  163.7 0.0 copy-start.1
  163.7 1.7 %copy.16 = bf16[1,1,32,4096]{3,2,1,0:T(8,128)(2,1)} copy(bf16[1,1,32,4096]{3,2,1,0:T(8,128)(2,1)} %bitcast.12) | data formatting | bytes 524288
  165.4 0.0 copy-done.1
  165.5 0.0 copy-start
  165.5 0.7 copy.17
  166.2 0.3 copy-done
  166.5 0.7 copy.18
Async XLA Ops:
  163.7 1.7 %copy-start.1 = (bf16[32,4096]{1,0:T(8,128)(2,1)S(1)}, bf16[32,4096]{1,0:T(8,128)(2,1)}, u32[]{:S(2)}) copy-start(bf16[32,4096]{1,0:T(8,128)(2,1)} %get-tuple-element.7) | copy-start | bytes 786436
  165.5 1.0 copy-start

commit v2 on v1

v2 whole, which is shorter than its diff:
```python
from types import SimpleNamespace

import jax
import jax.numpy as jnp
from jax import lax
from jax.experimental import pallas as pl
from jax.experimental.pallas import tpu as pltpu
from jax.sharding import PartitionSpec as P

MESH = pl.DeviceIdType.MESH
BF = jnp.bfloat16
F32 = jnp.float32

NX, NY, NZ = 4, 4, 8
NXY = NX * NY
D = 4096
DK = 256
COLS = 512
HEADS = COLS // DK
ROWS = 32
EROWS = 16
SL = D // NY
N = 128
EPS = 1e-06
SCALE = DK ** (-0.5)
STAT = 1.0 / (D * SCALE)
Q, K, V, O = range(4)
ORDER = (0, 1, 3, 2)


def vm(*shape, dtype=BF):
    return pltpu.VMEM(shape, dtype)


BUFFERS = dict(
    wq=vm(NZ, N, COLS),
    wk=vm(NZ, N, COLS),
    wv=vm(NZ, N, COLS),
    wo=vm(NZ, COLS, N),
    dec=vm(ROWS, D),
    enc_in=vm(EROWS, D),
    cot=vm(ROWS, D),
    gain_in=vm(1, D, dtype=F32),
    dseg=vm(1, N, dtype=jnp.int32),
    eseg=vm(1, N, dtype=jnp.int32),
    esl=vm(NY, EROWS, SL),
    enc=vm(2 * NXY, EROWS, SL),
    sl=vm(NY, ROWS, SL),
    a0=vm(NXY, ROWS, SL),
    a1=vm(NXY, ROWS, SL),
    dsl=vm(NY, ROWS, SL),
    x0=vm(NY, ROWS, SL),
    c0=vm(NY, ROWS, SL),
    x1=vm(NY, ROWS, SL),
    t1=vm(NY, ROWS, SL),
    t2=vm(NY, ROWS, SL),
    inv0s=vm(ROWS, N, dtype=F32),
    inv0=vm(NY, ROWS, N, dtype=F32),
    inv1=vm(NY, ROWS, N, dtype=F32),
    invx=vm(NX, ROWS, N, dtype=F32),
    gain=vm(8, SL, dtype=F32),
    gain_far=vm(8, SL, dtype=F32),
    mask=vm(N, N, dtype=F32),
    prob=vm(HEADS, N, N, dtype=F32),
    sgt=vm(HEADS, N, N),
    pt=vm(HEADS, N, N),
    q=vm(N, COLS),
    k=vm(N, COLS),
    v=vm(N, COLS),
    ag=vm(N, COLS),
    own_q=vm(N, COLS, dtype=F32),
    own_k=vm(N, COLS, dtype=F32),
    own_v=vm(N, COLS, dtype=F32),
    own_ag=vm(N, COLS, dtype=F32),
    s_q=vm(NY, N, COLS),
    s_k=vm(NY, N, COLS),
    s_v=vm(NY, N, COLS),
    s_ag=vm(NY, N, COLS),
    r_q=vm(NY, N, COLS),
    r_k=vm(NY, N, COLS),
    r_v=vm(NY, N, COLS),
    r_ag=vm(NY, N, COLS),
    at=vm(NY, N, COLS),
    qg=vm(NY, N, COLS),
    kg=vm(NY, N, COLS),
    vg=vm(NY, N, COLS),
    sxa=vm(NXY, ROWS, SL),
    sxb=vm(NXY, ROWS, SL),
    rxa=vm(NXY, ROWS, SL),
    rxb=vm(NXY, ROWS, SL),
    ss=vm(NY, NY, ROWS, N, dtype=F32),
    sp=vm(NX, ROWS, N, dtype=F32),
    spr1=vm(NX, ROWS, N, dtype=F32),
    spr0=vm(NX, ROWS, N, dtype=F32),
    sall1=vm(NY, ROWS, N, dtype=F32),
    sall0=vm(NY, ROWS, N, dtype=F32),
    por=vm(NY, ROWS, SL),
    sgr=vm(NY, ROWS, SL),
    mgs=vm(2 * NXY, EROWS, SL),
    mgc=vm(2 * NXY, EROWS, SL),
    rm=vm(NXY, EROWS, SL),
    mos=vm(NY, EROWS, SL),
    mo=vm(NY, EROWS, SL),
)

COPIES = dict(
    ring_q=(2, 4),
    ring_k=(2, 4),
    ring_v=(2, 4),
    ring_o=(2, 4),
    enc=(1,),
    sl=(1,),
    dsl=(1,),
    inv0=(1,),
    gain=(1,),
    ehalf=(1,),
    c0=(1,),
    pq=(1,),
    pk=(1,),
    pv=(1,),
    pag=(1,),
    at=(NY,),
    qg=(NY,),
    kg=(NY,),
    vg=(NY,),
    xa=(NY,),
    xb=(NY,),
    a1=(NY,),
    ss=(1,),
    invx=(1,),
    inv1=(1,),
    x1=(1,),
    spr1=(1,),
    spr0=(1,),
    sall1=(1,),
    sall0=(1,),
    por=(1,),
    por1=(1,),
    sgr=(1,),
    sgr0=(1,),
    mgc=(NY,),
    rm=(NY,),
    mo=(1,),
)
LOCAL = 13


def nn(a, b):
    return jnp.dot(a, b, preferred_element_type=F32)


def nt(a, b):
    return lax.dot_general(a, b, (((1,), (1,)), ((), ())), preferred_element_type=F32)


def kernel(*refs):
    dec, enc_in, dseg, eseg, gain_in, wq_in, wk_in, wv_in, wo_in, cot = refs[:10]
    out_p, out_s, out_m = refs[10:13]
    scratch = refs[13:]
    b = SimpleNamespace(**dict(zip(BUFFERS, scratch)))
    rest = scratch[len(BUFFERS) :]
    send_sems, local_sems, go = rest[len(COPIES) :]
    c = SimpleNamespace(**{n: (r, i) for i, (n, r) in enumerate(zip(COPIES, rest))})

    s = lax.axis_index("section")
    x = lax.axis_index("mp")
    dp = lax.axis_index("dp")
    y = dp % NY
    z = dp // NY
    far = 1 - s

    def dev(sec, xx, yy, zz=None):
        return {"section": sec, "mp": xx, "dp": (z if zz is None else zz) * NY + yy}

    here = dev(s, x, y)

    def copy(step, src, dst, at, device):
        return pltpu.make_async_remote_copy(
            src_ref=src,
            dst_ref=dst,
            send_sem=send_sems.at[step[1]],
            recv_sem=step[0].at[at],
            device_id=device,
            device_id_type=MESH,
        )

    def got(step, ref, at=0):
        copy(step, ref, ref, at, here).wait_recv()

    def sent(step, ref):
        first = (0,) * len(step[0].shape)
        copy(step, ref, ref, first, here).wait_send()

    def each(lo, hi, body):
        lax.fori_loop(lo, hi, lambda i, carry: (body(i), carry)[1], 0)

    def by_distance(i):
        return i + (i // 2) * (5 - 2 * i)

    def near(k):
        return (y + by_distance(k)) % NY

    def y_send(step, src_of, dst, sec, lo, at=None):
        def one(k):
            yp = (y + k) % NY
            copy(step, src_of(yp), dst.at[y], 0 if at is None else at, dev(sec, x, yp)).start()

        each(lo, NY, one)

    def x_send(step, src_of, dst, sec, lo, at=0):
        def one(k):
            xp = (x + k) % NX
            copy(step, src_of(xp), dst, at, dev(sec, xp, y)).start()

        each(lo, NX, one)

    weights = (b.wq, b.wk, b.wv, b.wo)
    rings = (c.ring_q, c.ring_k, c.ring_v, c.ring_o)

    def part(w, slot, step, way):
        ref = weights[w]
        if step < 3:
            return ref.at[slot]
        half = ref.shape[1] // 2
        return ref.at[slot, pl.ds(way * half, half)]

    def ring_send(w, step):
        for way in range(2):
            slot = (z + NZ - step) % NZ if way == 0 else (z + step) % NZ
            to = (z + 1) % NZ if way == 0 else (z + NZ - 1) % NZ
            ref = part(w, slot, step, way)
            copy(rings[w], ref, ref, (way, step), dev(s, x, y, to)).start()

    def ring_got(w, step):
        for way in range(2):
            slot = (z + NZ - 1 - step) % NZ if way == 0 else (z + 1 + step) % NZ
            got(rings[w], part(w, slot, step, way), (way, step))

    def ring_next(step, *ws):
        for w in ws:
            ring_got(w, step - 1)
            ring_send(w, step)

    barrier = pltpu.get_barrier_semaphore()

    def hello(device):
        pl.semaphore_signal(barrier, inc=1, device_id=device, device_id_type=MESH)

    def hello_xy(k):
        t = (NX * y + x + k) % NXY
        hello(dev(s, t % NX, t // NX))

    each(1, NXY, hello_xy)
    hello(dev(s, x, y, (z + 1) % NZ))
    hello(dev(s, x, y, (z + NZ - 1) % NZ))
    each(0, NX, lambda k: hello(dev(far, (x + k) % NX, y)))
    each(1, NY, lambda k: hello(dev(far, x, (y + k) % NY)))

    def local(src, dst, i):
        return pltpu.make_async_copy(src, dst, local_sems.at[i])

    loads = [
        local(src, dst, i)
        for i, (src, dst) in enumerate(
            (
                (dec, b.dec),
                (gain_in, b.gain_in),
                (enc_in, b.enc_in),
                (dseg, b.dseg),
                (eseg, b.eseg),
                (cot, b.cot),
                (wq_in, b.wq.at[z]),
                (wk_in, b.wk.at[z]),
                (wv_in, b.wv.at[z]),
                (wo_in, b.wo.at[z]),
            )
        )
    ]
    for load in loads:
        load.start()
    for load in loads:
        load.wait()

    def pick(value, yp):
        return jnp.concatenate(
            [value[:, (NY * f + yp) * N : (NY * f + yp + 1) * N] for f in range(NZ)], axis=1
        )

    rows_in = b.dec[...]
    enc_rows = b.enc_in[...]

    @pl.when(s == 0)
    def _():
        wide = rows_in.astype(F32)
        inverse = lax.rsqrt(jnp.mean(wide * wide, axis=-1, keepdims=True) + EPS)
        inv_tile = jnp.broadcast_to(inverse, (ROWS, N))
        b.inv0s[...] = inv_tile
        b.inv0[y] = inv_tile
        hidden = (wide * inverse * b.gain_in[...]).astype(BF)
        for yp in range(NY):
            b.sl[yp] = pick(hidden, yp)

    @pl.when(s == 1)
    def _():
        value = b.cot[...]
        for yp in range(NY):
            b.sl[yp] = pick(value, yp)

    for yp in range(NY):
        b.dsl[yp] = pick(rows_in, yp)
        b.esl[yp] = pick(enc_rows, yp)
    b.a0[NX * y + x] = b.sl[y]
    b.x0[y] = b.dsl[y]
    b.enc[(2 * y + s) * NX + x] = b.esl[y]
    for f in range(NZ):
        own_gain = b.gain_in[:, pl.ds(pl.multiple_of((NY * f + y) * N, N), N)]
        b.gain[:, f * N : (f + 1) * N] = jnp.broadcast_to(own_gain, (8, N))
    dec_ids = jnp.broadcast_to(b.dseg[...].astype(F32), (N, N)).T
    enc_ids = jnp.broadcast_to(b.eseg[...].astype(F32), (N, N))
    b.mask[...] = jnp.where(dec_ids == enc_ids, 1.0, 0.0)

    pl.semaphore_wait(barrier, NXY - 1 + 2 + NX + NY - 1)

    def xy_start(step, src, dst):
        def one(k):
            t = (NX * y + x + k) % NXY
            copy(step, src.at[t // NX], dst, 0, dev(s, t % NX, t // NX)).start()

        each(1, NXY, one)

    def enc_start():
        xy_start(c.enc, b.esl, b.enc.at[(2 * y + s) * NX + x])

    def sl_start():
        xy_start(c.sl, b.sl, b.a0.at[NX * y + x])

    def small_start():
        copy(c.gain, b.gain, b.gain_far, 0, dev(far, x, y)).start()
        y_send(c.dsl, lambda i: b.dsl.at[i], b.x0, s, 1)

    def enc_half():
        got(c.enc, b.enc.at[pl.ds(0, NXY - 1)])
        for yp in range(NY):
            block = b.enc.at[pl.ds((2 * yp + s) * NX, NX)]
            copy(c.ehalf, block, block, 0, dev(far, x, y)).start()

    def enc_whole():
        got(c.ehalf, b.enc.at[pl.ds(0, NXY)])

    def sl_got():
        got(c.sl, b.a0.at[pl.ds(0, NXY - 1)])

    def times(w, a):
        return nn(a, weights[w][...].reshape(NZ * N, COLS))

    def pair(p):
        return jnp.concatenate([b.wo[2 * p], b.wo[2 * p + 1]], axis=1)

    def times_out_t(a):
        total = nt(a[:, : 2 * N], pair(0))
        for p in range(1, NZ // 2):
            total += nt(a[:, 2 * N * p : 2 * N * (p + 1)], pair(p))
        return total

    def dec_rows(buffer):
        return lambda yp: buffer[pl.ds(NX * yp, NX)].reshape(N, SL)

    def enc_group(yp):
        return b.enc[pl.ds(2 * NX * yp, 2 * NX)].reshape(N, SL)

    def project(step, rows_of, product, stage, landing, own, arrived=None):
        def one(k):
            yp = near(k)
            if arrived is not None:
                arrived(yp)
            stage[yp] = product(rows_of(yp)).astype(BF)
            copy(step, stage.at[yp], landing.at[y], 0, dev(s, x, yp)).start()

        if arrived is not None:
            arrived(y)
            own[...] = product(rows_of(y))
            each(1, NY, one)
        else:
            each(1, NY, one)
            own[...] = product(rows_of(y))

    def projected(step, landing, own):
        got(step, landing.at[pl.ds(0, NY - 1)])
        total = own[...]
        for k in range(1, NY):
            total += landing[(y + k) % NY].astype(F32)
        return total

    def head(value, h):
        return value[:, h * DK : (h + 1) * DK]

    def probabilities():
        for h in range(HEADS):
            scores = nt(head(b.q, h), head(b.k, h))
            scores = jnp.where(b.mask[...] > 0.5, scores, -1e30)
            top = jnp.max(scores, axis=-1, keepdims=True)
            e = jnp.exp(scores - top)
            b.prob[h] = e / jnp.sum(e, axis=-1, keepdims=True)

    def gather_y(step, buffer):
        def one(k):
            copy(step, buffer.at[y], buffer.at[y], y, dev(s, x, near(k))).start()

        each(1, NY, one)

    def attend():
        b.at[y] = jnp.concatenate(
            [nn(b.prob[h].astype(BF), head(b.v, h)) for h in range(HEADS)], axis=1
        ).astype(BF)
        gather_y(c.at, b.at)

    def query_gradient():
        grads = []
        for h in range(HEADS):
            prob = b.prob[h]
            prob_grad = nt(head(b.ag, h), head(b.v, h))
            score_grad = prob * (prob_grad - jnp.sum(prob_grad * prob, axis=-1, keepdims=True))
            b.sgt[h] = score_grad.T.astype(BF)
            grads.append(nn(score_grad.astype(BF), head(b.k, h)) * SCALE)
        low = jnp.concatenate(grads, axis=1).astype(BF)
        b.qg[y] = low
        gather_y(c.qg, b.qg)
        both = low.astype(F32) * b.q[...].astype(F32)
        lanes = both[:, :N]
        for f in range(1, COLS // N):
            lanes += both[:, f * N : (f + 1) * N]
        b.sp[...] = lanes.reshape(NX, ROWS, N)

    def key_value_gradients():
        for h in range(HEADS):
            b.pt[h] = b.prob[h].T.astype(BF)
        b.kg[y] = jnp.concatenate(
            [nn(b.sgt[h], head(b.q, h)) for h in range(HEADS)], axis=1
        ).astype(BF)
        gather_y(c.kg, b.kg)
        b.vg[y] = jnp.concatenate(
            [nn(b.pt[h], head(b.ag, h)) for h in range(HEADS)], axis=1
        ).astype(BF)
        gather_y(c.vg, b.vg)

    def update_rows(yp, stage):
        a = b.at[yp]
        for p in range(NZ // 2):
            part_out = nn(a, pair(p)).astype(BF).reshape(NX, ROWS, 2 * N)
            stage[pl.ds(NX * yp, NX), :, 2 * N * p : 2 * N * (p + 1)] = part_out

    def hidden_rows(yp, stage):
        a = b.qg[yp]
        for p in range(NZ // 2):
            block = b.wq[2 * p : 2 * p + 2].reshape(2 * N, COLS)
            part_out = nt(a, block).astype(BF).reshape(NX, ROWS, 2 * N)
            stage[pl.ds(NX * yp, NX), :, 2 * N * p : 2 * N * (p + 1)] = part_out

    def scatter_x(step, source_step, source, rows_into, stage, landing, sec, keep):
        def one(k):
            yp = near(k)

            @pl.when(k > 0)
            def _():
                got(source_step, source.at[yp], yp)

            rows_into(yp, stage)
            x_send(
                step,
                lambda xp: stage.at[NX * yp + xp],
                landing.at[NX * yp + x],
                sec,
                1 if keep else 0,
                yp,
            )
            if keep:
                landing[NX * yp + x] = stage[NX * yp + x]

        each(0, NY, one)

    def x_got(step, landing, yp, blocks):
        got(step, landing.at[pl.ds(NX * yp, blocks)], yp)

    def sum_x(landing, yp):
        total = landing[NX * yp].astype(F32)
        for i in range(1, NX):
            total += landing[NX * yp + i].astype(F32)
        return total

    def gather_x(yp):
        block = b.a1.at[NX * yp + x]
        x_send(c.a1, lambda xp: block, block, s, 1, yp)

    def a1_got(yp):
        x_got(c.a1, b.a1, yp, NX - 1)

    def across(tile):
        return jnp.concatenate([tile] * (SL // N), axis=1)

    def send_stat(step, landing, keep):
        x_send(step, lambda xp: b.sp.at[xp], landing.at[x], 0, 1 if keep else 0)
        if keep:
            landing[x] = b.sp[x]

    def share_stat(step, landing, result, step_out, blocks):
        got(step, landing.at[pl.ds(0, blocks)])
        lanes = landing[0] + landing[1] + landing[2] + landing[3]
        result[y] = jnp.broadcast_to(jnp.sum(lanes, axis=-1, keepdims=True), (ROWS, N))
        y_send(step_out, lambda i: result.at[y], result, 0, 1)

    def norm_gradient(yp, landing, gain_ref, rows, inv_ref, stat_ref, grad):
        u = sum_x(landing, yp) * gain_ref[0:1, :]
        inv = inv_ref[yp]
        coef = inv * inv * stat_ref[yp] * STAT
        wide_rows = rows[yp].astype(F32)
        return (grad[yp].astype(F32) + across(inv) * u - wide_rows * across(coef)).astype(BF)

    def memory_rows(yp, into):
        key = b.kg[yp]
        value = b.vg[yp]
        for p in range(NZ // 2):
            wk_block = b.wk[2 * p : 2 * p + 2].reshape(2 * N, COLS)
            wv_block = b.wv[2 * p : 2 * p + 2].reshape(2 * N, COLS)
            block = (nt(key, wk_block) + nt(value, wv_block)).reshape(2 * NX, EROWS, 2 * N)
            into(slice(2 * N * p, 2 * N * (p + 1)), block)

    def kv_got(k):
        yp = near(k)

        @pl.when(k > 0)
        def _():
            got(c.kg, b.kg.at[yp], yp)
            got(c.vg, b.vg.at[yp], yp)

        return yp

    @pl.when(s == 0)
    def _():
        ring_send(Q, 0)
        ring_send(K, 0)
        ring_send(V, 0)
        enc_start()
        sl_start()
        ring_next(1, Q, K, V)
        ring_send(O, 0)
        small_start()
        y_send(c.inv0, lambda i: b.inv0s, b.inv0, 0, 1)
        ring_next(2, Q, K, V)
        ring_next(1, O)
        enc_half()
        ring_next(3, Q, K, V)
        ring_next(2, O)
        sl_got()
        ring_got(Q, 3)
        project(c.pq, dec_rows(b.a0), lambda a: times(Q, a), b.s_q, b.r_q, b.own_q)
        ring_next(3, O)
        pl.semaphore_signal(go, inc=1, device_id=dev(1, x, y), device_id_type=MESH)
        enc_whole()
        ring_got(K, 3)
        project(c.pk, enc_group, lambda a: times(K, a), b.s_k, b.r_k, b.own_k)
        ring_got(V, 3)
        project(c.pv, enc_group, lambda a: times(V, a), b.s_v, b.r_v, b.own_v)
        b.q[...] = (projected(c.pq, b.r_q, b.own_q) * SCALE).astype(BF)
        b.k[...] = projected(c.pk, b.r_k, b.own_k).astype(BF)
        probabilities()
        b.v[...] = projected(c.pv, b.r_v, b.own_v).astype(BF)
        attend()
        ring_got(O, 3)
        scatter_x(c.xa, c.at, b.at, update_rows, b.sxa, b.rxa, 1, False)

        got(c.gain, b.gain_far)
        got(c.c0, b.c0)
        got(c.dsl, b.x0.at[pl.ds(0, NY - 1)])
        got(c.inv0, b.inv0.at[pl.ds(0, NY - 1)])
        got(c.x1, b.x1)
        got(c.inv1, b.inv1)
        share_stat(c.spr1, b.spr1, b.sall1, c.sall1, NX)

        def grad_one(k):
            yp = near(k)
            x_got(c.xa, b.rxa, yp, NX)

            @pl.when(k == 1)
            def _():
                got(c.sall1, b.sall1.at[pl.ds(0, NY - 1)])

            g = norm_gradient(yp, b.rxa, b.gain_far, b.x1, b.inv1, b.sall1, b.c0)
            b.t1[yp] = g
            b.a1[NX * yp + x] = g
            gather_x(yp)

        each(0, NY, grad_one)
        y_send(c.sgr, lambda i: b.t1.at[i], b.sgr, 1, 0)

        project(c.pag, dec_rows(b.a1), times_out_t, b.s_ag, b.r_ag, b.own_ag, a1_got)
        b.ag[...] = projected(c.pag, b.r_ag, b.own_ag).astype(BF)
        query_gradient()
        send_stat(c.spr0, b.spr0, True)
        key_value_gradients()
        scatter_x(c.xb, c.qg, b.qg, hidden_rows, b.sxb, b.rxb, 0, True)
        share_stat(c.spr0, b.spr0, b.sall0, c.sall0, NX - 1)

        def memory_zero(k):
            yp = kv_got(k)
            far_rows = b.mgc.at[pl.ds(2 * NX * yp, 2 * NX)]
            got(c.mgc, far_rows, yp)

            def into(lanes, block):
                total = block + far_rows[:, :, lanes].astype(F32)
                b.mgs[pl.ds(2 * NX * yp, 2 * NX), :, lanes] = total.astype(BF)

            memory_rows(yp, into)
            for sec in range(2):
                x_send(
                    c.rm,
                    lambda xp, sec=sec: b.mgs.at[(2 * yp + sec) * NX + xp],
                    b.rm.at[NX * yp + x],
                    sec,
                    1 - sec,
                    yp,
                )
            b.rm[NX * yp + x] = b.mgs[2 * NX * yp + x]

        each(0, NY, memory_zero)

        def grad_zero(k):
            yp = near(k)
            x_got(c.xb, b.rxb, yp, NX - 1)

            @pl.when(k == 1)
            def _():
                got(c.sall0, b.sall0.at[pl.ds(0, NY - 1)])

            b.t2[yp] = norm_gradient(yp, b.rxb, b.gain, b.x0, b.inv0, b.sall0, b.t1)

            @pl.when(k > 0)
            def _():
                copy(c.sgr0, b.t2.at[yp], b.sgr.at[y], 0, dev(0, x, yp)).start()

        each(0, NY, grad_zero)
        b.sgr[y] = b.t2[y]

    @pl.when(s == 1)
    def _():
        enc_start()
        small_start()
        enc_half()
        got(c.dsl, b.x0.at[pl.ds(0, NY - 1)])
        got(c.gain, b.gain_far)
        enc_whole()
        pl.semaphore_wait(go, 1)
        ring_send(K, 0)
        ring_send(V, 0)
        ring_send(O, 0)
        sl_start()
        ring_next(1, K, V, O)
        ring_send(Q, 0)
        ring_next(2, K, V, O)
        ring_next(1, Q)
        ring_next(3, K, V, O)
        ring_next(2, Q)
        ring_got(K, 3)
        project(c.pk, enc_group, lambda a: times(K, a), b.s_k, b.r_k, b.own_k)
        ring_next(3, Q)
        ring_got(V, 3)
        project(c.pv, enc_group, lambda a: times(V, a), b.s_v, b.r_v, b.own_v)
        sl_got()
        for yp in range(NY):
            copy(c.c0, b.a0.at[NX * yp + x], b.c0.at[yp], 0, dev(0, x, y)).start()
        ring_got(O, 3)
        project(c.pag, dec_rows(b.a0), times_out_t, b.s_ag, b.r_ag, b.own_ag)
        b.k[...] = projected(c.pk, b.r_k, b.own_k).astype(BF)
        b.v[...] = projected(c.pv, b.r_v, b.own_v).astype(BF)
        b.ag[...] = projected(c.pag, b.r_ag, b.own_ag).astype(BF)
        ring_got(Q, 3)

        def stream_one(k):
            yp = near(k)
            x_got(c.xa, b.rxa, yp, NX)
            rows = (b.x0[yp].astype(F32) + sum_x(b.rxa, yp)).astype(BF)
            b.x1[yp] = rows
            rows = rows.astype(F32)
            b.a1[NX * yp + x] = (rows * b.gain[0:1, :]).astype(BF)
            gather_x(yp)
            squares = rows * rows
            lanes = squares[:, :N]
            for f in range(1, SL // N):
                lanes += squares[:, f * N : (f + 1) * N]
            b.ss[y, yp] = lanes

        each(0, NY, stream_one)
        y_send(c.ss, lambda i: b.ss.at[y], b.ss, 1, 1)
        copy(c.x1, b.x1, b.x1, 0, dev(0, x, y)).start()
        y_send(c.por, lambda i: b.x1.at[i], b.por, 0, 0)
        got(c.ss, b.ss.at[pl.ds(0, NY - 1)])

        def inverse_one(yp):
            lanes = b.ss[0, yp] + b.ss[1, yp] + b.ss[2, yp] + b.ss[3, yp]
            inv = lax.rsqrt(jnp.sum(lanes, axis=-1, keepdims=True) * (1.0 / D) + EPS)
            b.inv1[yp] = jnp.broadcast_to(inv, (ROWS, N))

        each(0, NY, inverse_one)
        b.invx[x] = b.inv1[y]
        x_send(c.invx, lambda xp: b.inv1.at[y], b.invx.at[x], 1, 1)
        copy(c.inv1, b.inv1, b.inv1, 0, dev(0, x, y)).start()
        project(c.pq, dec_rows(b.a1), lambda a: times(Q, a), b.s_q, b.r_q, b.own_q, a1_got)
        got(c.invx, b.invx.at[pl.ds(0, NX - 1)])
        row_scale = b.invx[...].reshape(N, N) * SCALE
        row_scale = jnp.concatenate([row_scale] * (COLS // N), axis=1)
        b.q[...] = (projected(c.pq, b.r_q, b.own_q) * row_scale).astype(BF)
        probabilities()
        query_gradient()
        send_stat(c.spr1, b.spr1, False)
        scatter_x(c.xa, c.qg, b.qg, hidden_rows, b.sxa, b.rxa, 0, False)

        key_value_gradients()

        def memory_one(k):
            yp = kv_got(k)

            def into(lanes, block):
                b.mgs[pl.ds(2 * NX * yp, 2 * NX), :, lanes] = block.astype(BF)

            memory_rows(yp, into)
            rows = pl.ds(2 * NX * yp, 2 * NX)
            copy(c.mgc, b.mgs.at[rows], b.mgc.at[rows], yp, dev(0, x, y)).start()

        each(0, NY, memory_one)
        attend()
        scatter_x(c.xb, c.at, b.at, update_rows, b.sxb, b.rxb, 1, True)

        def output_one(k):
            yp = near(k)
            x_got(c.xb, b.rxb, yp, NX - 1)
            b.t2[yp] = (b.x1[yp].astype(F32) + sum_x(b.rxb, yp)).astype(BF)

        each(0, NY, output_one)
        y_send(c.por1, lambda i: b.t2.at[i], b.por, 1, 1)
        b.por[y] = b.t2[y]

    store_p = local(b.por, out_p, 10)
    store_s = local(b.sgr, out_s, 11)
    store_m = local(b.mo, out_m, 12)

    @pl.when(s == 0)
    def _():
        got(c.por, b.por)

    @pl.when(s == 1)
    def _():
        got(c.por1, b.por.at[pl.ds(0, NY - 1)])
        got(c.sgr, b.sgr)
        store_s.start()

    store_p.start()

    def memory_sum(k):
        yp = near(k)

        @pl.when(s == 0)
        def _():
            x_got(c.rm, b.rm, yp, NX - 1)

        @pl.when(s == 1)
        def _():
            x_got(c.rm, b.rm, yp, NX)

        b.mos[yp] = sum_x(b.rm, yp).astype(BF)

        @pl.when(k > 0)
        def _():
            copy(c.mo, b.mos.at[yp], b.mo.at[y], 0, dev(s, x, yp)).start()

    each(0, NY, memory_sum)
    b.mo[y] = b.mos[y]

    @pl.when(s == 0)
    def _():
        got(c.sgr0, b.sgr.at[pl.ds(0, NY - 1)])
        store_s.start()

    got(c.mo, b.mo.at[pl.ds(0, NY - 1)])
    store_m.start()

    three = pl.ds(0, NY - 1)
    for w in range(4):
        sent(rings[w], weights[w].at[pl.ds(0, NZ - 1)])
    sent(c.sl, b.a0.at[pl.ds(0, NXY - 1)])
    sent(c.enc, b.enc.at[pl.ds(0, NXY - 1)])
    sent(c.ehalf, b.enc.at[pl.ds(0, NXY)])
    sent(c.dsl, b.dsl.at[three])
    sent(c.gain, b.gain)
    for step in (c.pq, c.pk, c.pv, c.pag, c.at, c.qg, c.kg, c.vg):
        sent(step, b.s_q.at[three])
    sent(c.a1, b.a1.at[pl.ds(0, NXY - NY)])
    sent(c.xa, b.sxa)
    sent(c.xb, b.sxb.at[pl.ds(0, NXY - NY)])
    sent(c.mo, b.mos.at[three])

    @pl.when(s == 0)
    def _():
        sent(c.inv0, b.inv0.at[three])
        sent(c.sall1, b.sall1.at[three])
        sent(c.sall0, b.sall0.at[three])
        sent(c.spr0, b.sp.at[three])
        sent(c.sgr, b.t1)
        sent(c.sgr0, b.t2.at[three])
        sent(c.rm, b.mgs.at[pl.ds(0, 2 * NXY - NY)])

    @pl.when(s == 1)
    def _():
        sent(c.c0, b.c0)
        sent(c.x1, b.x1)
        sent(c.inv1, b.inv1)
        sent(c.mgc, b.mgs)
        sent(c.por, b.x1)
        sent(c.por1, b.t2.at[three])
        sent(c.ss, b.ss.at[three])
        sent(c.invx, b.invx.at[three])
        sent(c.spr1, b.sp)

    store_p.wait()
    store_s.wait()
    store_m.wait()


def assemble(phase, stream, memory, out_p, out_s, out_m):
    for source, out in ((phase, out_p), (stream, out_s), (memory, out_m)):
        for yp in range(NY):
            value = source[yp]
            for f in range(NZ):
                at = (NY * f + yp) * N
                out[:, at : at + N] = value[:, f * N : (f + 1) * N].astype(out.dtype)


def body(*args):
    dec, enc, dseg, eseg, gain, wq, wk, wv, wo, cot = args
    parts = pl.pallas_call(
        kernel,
        out_shape=(
            jax.ShapeDtypeStruct((NY, ROWS, SL), BF),
            jax.ShapeDtypeStruct((NY, ROWS, SL), BF),
            jax.ShapeDtypeStruct((NY, EROWS, SL), BF),
        ),
        in_specs=[pl.BlockSpec(memory_space=pl.ANY)] * 10,
        out_specs=(pl.BlockSpec(memory_space=pl.ANY),) * 3,
        scratch_shapes=list(BUFFERS.values())
        + [pltpu.SemaphoreType.DMA(shape) for shape in COPIES.values()]
        + [
            pltpu.SemaphoreType.DMA((len(COPIES),)),
            pltpu.SemaphoreType.DMA((LOCAL,)),
            pltpu.SemaphoreType.REGULAR,
        ],
        compiler_params=pltpu.CompilerParams(
            collective_id=0, has_side_effects=True, vmem_limit_bytes=56 * 2**20
        ),
        cost_estimate=pl.CostEstimate(
            flops=16 * 2**30, bytes_accessed=4 * 2**20, transcendentals=2**16
        ),
        name="decoder_phases",
    )(dec[0], enc[0], dseg, eseg, gain, wq[0], wk[0], wv[0], wo[0], cot[0])
    phase, stream, memory = pl.pallas_call(
        assemble,
        out_shape=(
            jax.ShapeDtypeStruct((ROWS, D), BF),
            jax.ShapeDtypeStruct((ROWS, D), BF),
            jax.ShapeDtypeStruct((EROWS, D), F32),
        ),
        in_specs=[pl.BlockSpec(memory_space=pltpu.VMEM)] * 3,
        out_specs=(pl.BlockSpec(memory_space=pltpu.VMEM),) * 3,
        name="assemble",
    )(*parts)
    return phase[None, None], stream[None, None], memory[None]


def solution(mesh):
    in_specs = (
        P("dp", "mp", None),
        P("dp", ("section", "mp"), None),
        P("dp", None),
        P("dp", None),
        P("section", None),
        P("section", "dp", "mp"),
        P("section", "dp", "mp"),
        P("section", "dp", "mp"),
        P("section", "mp", "dp"),
        P("dp", "mp", None),
    )
    out_specs = (
        P("section", "dp", "mp", None),
        P("section", "dp", "mp", None),
        P("dp", ("section", "mp"), None),
    )
    return jax.shard_map(body, mesh=mesh, in_specs=in_specs, out_specs=out_specs, check_vma=False)
```

time: 167 us -> 131 us (0.78)
  Pallas kernels: 163 us -> 130 us
  local copies, waits for them, and re-layouts: 3.46 us -> 0 us
    pallas_call x1 -> x2, Pallas kernels: 163 us -> 130 us  [the longest x1 128 us: body(): pl.pallas_call(kernel, out_shape=(jax.ShapeDtypeStruct((NY, ROWS, SL), BF...]
    unnamed x7 -> x0, local copies, waits for them, and re-layouts: 3.46 us -> none
where the time goes in v2:
time: 131 us
  Pallas kernels  130 us (99%)
    pallas_call x1, Pallas kernels, body(): pl.pallas_call(kernel, out_shape=(jax.ShapeDtypeStruct((NY, ROWS, SL), BF...  128 us

profile of v2, /device:TPU:1, one launch (start us, length us, event | category | flops | bytes accessed | tf_op | source)
XLA Modules:
  0.0 130.8 jit_solution(4486743172469726334)
XLA Ops:
  0.6 128.2 %decoder_phases.1 = (bf16[4,32,1024]{2,1,0:T(8,128)(2,1)}, bf16[4,32,1024]{2,1,0:T(8,128)(2,1)}, bf16[4,16,1024]{2,1,0:T(8,128)(2,1)}) custom-call(bf16[32,4096]{1,0:T(8,128)(2,1)} %bitcast.10, bf16[16,4096]{1,0:T(8,128)(2,1)} %bitcast.15, s32[1,128]{1,0:T(1,128)} %refs_2_.1, s32[1,128]{1,0:T(1,128)} %refs_3_.1, f32[1,4096]{1,0:T(1,128)} %refs_4_.1, ...), custom_call_target="tpu_custom_call" | custom-call | flops 17179869184 | bytes 4194304 | tf_op jit(solution)/shard_map/decoder_phases/pallas_call | solution.py:838
  128.8 2.0 %assemble.1 = (bf16[32,4096]{1,0:T(8,128)(2,1)}, bf16[32,4096]{1,0:T(8,128)(2,1)}, f32[16,4096]{1,0:T(8,128)}) custom-call(bf16[4,32,1024]{2,1,0:T(8,128)(2,1)} %get-tuple-element.9.phase, bf16[4,32,1024]{2,1,0:T(8,128)(2,1)} %get-tuple-element.10.stream, bf16[4,16,1024]{2,1,0:T(8,128)(2,1)} %get-tuple-element.11.memory), custom_call_target="tpu_custom_call" | custom-call | tf_op jit(solution)/shard_map/assemble/pallas_call | solution.py:862

commit v3 on v2

--- a/solution.py
+++ b/solution.py
@@ -62,6 +62,7 @@
     gain_far=vm(8, SL, dtype=F32),
     mask=vm(N, N, dtype=F32),
     prob=vm(HEADS, N, N, dtype=F32),
+    pg=vm(HEADS, N, N, dtype=F32),
     sgt=vm(HEADS, N, N),
     pt=vm(HEADS, N, N),
     q=vm(N, COLS),
@@ -414,11 +415,15 @@
         ).astype(BF)
         gather_y(c.at, b.at)
 
+    def probability_gradient():
+        for h in range(HEADS):
+            b.pg[h] = nt(head(b.ag, h), head(b.v, h))
+
     def query_gradient():
         grads = []
         for h in range(HEADS):
             prob = b.prob[h]
-            prob_grad = nt(head(b.ag, h), head(b.v, h))
+            prob_grad = b.pg[h]
             score_grad = prob * (prob_grad - jnp.sum(prob_grad * prob, axis=-1, keepdims=True))
             b.sgt[h] = score_grad.T.astype(BF)
             grads.append(nn(score_grad.astype(BF), head(b.k, h)) * SCALE)
@@ -456,13 +461,15 @@
             part_out = nt(a, block).astype(BF).reshape(NX, ROWS, 2 * N)
             stage[pl.ds(NX * yp, NX), :, 2 * N * p : 2 * N * (p + 1)] = part_out
 
-    def scatter_x(step, source_step, source, rows_into, stage, landing, sec, keep):
+    def scatter_x(step, source_step, source, rows_into, stage, landing, sec, keep, then=None):
         def one(k):
             yp = near(k)
 
-            @pl.when(k > 0)
-            def _():
-                got(source_step, source.at[yp], yp)
+            if not isinstance(k, int):
+
+                @pl.when(k > 0)
+                def _():
+                    got(source_step, source.at[yp], yp)
 
             rows_into(yp, stage)
             x_send(
@@ -476,7 +483,12 @@
             if keep:
                 landing[NX * yp + x] = stage[NX * yp + x]
 
-        each(0, NY, one)
+        if then is None:
+            each(0, NY, one)
+        else:
+            one(0)
+            then()
+            each(1, NY, one)
 
     def x_got(step, landing, yp, blocks):
         got(step, landing.at[pl.ds(NX * yp, blocks)], yp)
@@ -536,28 +548,27 @@
 
     @pl.when(s == 0)
     def _():
-        ring_send(Q, 0)
-        ring_send(K, 0)
-        ring_send(V, 0)
+        for w in (Q, K, V):
+            ring_send(w, 0)
         enc_start()
         sl_start()
         ring_next(1, Q, K, V)
-        ring_send(O, 0)
         small_start()
         y_send(c.inv0, lambda i: b.inv0s, b.inv0, 0, 1)
         ring_next(2, Q, K, V)
-        ring_next(1, O)
+        ring_send(O, 0)
         enc_half()
         ring_next(3, Q, K, V)
-        ring_next(2, O)
+        pl.semaphore_signal(go, inc=1, device_id=dev(1, x, y), device_id_type=MESH)
+        ring_next(1, O)
         sl_got()
         ring_got(Q, 3)
         project(c.pq, dec_rows(b.a0), lambda a: times(Q, a), b.s_q, b.r_q, b.own_q)
-        ring_next(3, O)
-        pl.semaphore_signal(go, inc=1, device_id=dev(1, x, y), device_id_type=MESH)
+        ring_next(2, O)
         enc_whole()
         ring_got(K, 3)
         project(c.pk, enc_group, lambda a: times(K, a), b.s_k, b.r_k, b.own_k)
+        ring_next(3, O)
         ring_got(V, 3)
         project(c.pv, enc_group, lambda a: times(V, a), b.s_v, b.r_v, b.own_v)
         b.q[...] = (projected(c.pq, b.r_q, b.own_q) * SCALE).astype(BF)
@@ -594,10 +605,10 @@
 
         project(c.pag, dec_rows(b.a1), times_out_t, b.s_ag, b.r_ag, b.own_ag, a1_got)
         b.ag[...] = projected(c.pag, b.r_ag, b.own_ag).astype(BF)
+        probability_gradient()
         query_gradient()
         send_stat(c.spr0, b.spr0, True)
-        key_value_gradients()
-        scatter_x(c.xb, c.qg, b.qg, hidden_rows, b.sxb, b.rxb, 0, True)
+        scatter_x(c.xb, c.qg, b.qg, hidden_rows, b.sxb, b.rxb, 0, True, key_value_gradients)
         share_stat(c.spr0, b.spr0, b.sall0, c.sall0, NX - 1)
 
         def memory_zero(k):
@@ -648,20 +659,15 @@
         got(c.dsl, b.x0.at[pl.ds(0, NY - 1)])
         got(c.gain, b.gain_far)
         enc_whole()
+        sl_start()
         pl.semaphore_wait(go, 1)
-        ring_send(K, 0)
-        ring_send(V, 0)
-        ring_send(O, 0)
-        sl_start()
-        ring_next(1, K, V, O)
-        ring_send(Q, 0)
-        ring_next(2, K, V, O)
-        ring_next(1, Q)
-        ring_next(3, K, V, O)
-        ring_next(2, Q)
+        for w in (K, V, O, Q):
+            ring_send(w, 0)
+        ring_next(1, K, V, O, Q)
+        ring_next(2, K, V, O, Q)
+        ring_next(3, K, V, O, Q)
         ring_got(K, 3)
         project(c.pk, enc_group, lambda a: times(K, a), b.s_k, b.r_k, b.own_k)
-        ring_next(3, Q)
         ring_got(V, 3)
         project(c.pv, enc_group, lambda a: times(V, a), b.s_v, b.r_v, b.own_v)
         sl_got()
@@ -669,11 +675,6 @@
             copy(c.c0, b.a0.at[NX * yp + x], b.c0.at[yp], 0, dev(0, x, y)).start()
         ring_got(O, 3)
         project(c.pag, dec_rows(b.a0), times_out_t, b.s_ag, b.r_ag, b.own_ag)
-        b.k[...] = projected(c.pk, b.r_k, b.own_k).astype(BF)
-        b.v[...] = projected(c.pv, b.r_v, b.own_v).astype(BF)
-        b.ag[...] = projected(c.pag, b.r_ag, b.own_ag).astype(BF)
-        ring_got(Q, 3)
-
         def stream_one(k):
             yp = near(k)
             x_got(c.xa, b.rxa, yp, NX)
@@ -690,6 +691,12 @@
 
         each(0, NY, stream_one)
         y_send(c.ss, lambda i: b.ss.at[y], b.ss, 1, 1)
+        b.k[...] = projected(c.pk, b.r_k, b.own_k).astype(BF)
+        b.v[...] = projected(c.pv, b.r_v, b.own_v).astype(BF)
+        b.ag[...] = projected(c.pag, b.r_ag, b.own_ag).astype(BF)
+        probability_gradient()
+        ring_got(Q, 3)
+
         copy(c.x1, b.x1, b.x1, 0, dev(0, x, y)).start()
         y_send(c.por, lambda i: b.x1.at[i], b.por, 0, 0)
         got(c.ss, b.ss.at[pl.ds(0, NY - 1)])

time: 131 us -> 124 us (0.947)
  Pallas kernels: 130 us -> 123 us
    pallas_call x1, Pallas kernels: 128 us -> 121 us  [body(): pl.pallas_call(kernel, out_shape=(jax.ShapeDtypeStruct((NY, ROWS, SL), BF...]
where the time goes in v3:
time: 124 us; the launch traced here: 123 us
  Pallas kernels  123 us (99%)
    pallas_call x1, Pallas kernels, body(): pl.pallas_call(kernel, out_shape=(jax.ShapeDtypeStruct((NY, ROWS, SL), BF...  121 us

profile of v3, /device:TPU:1, one launch (start us, length us, event | category | flops | bytes accessed | tf_op | source)
XLA Modules:
  0.0 123.4 jit_solution(13578174257986768846)
XLA Ops:
  0.6 120.8 %decoder_phases.1 = (bf16[4,32,1024]{2,1,0:T(8,128)(2,1)}, bf16[4,32,1024]{2,1,0:T(8,128)(2,1)}, bf16[4,16,1024]{2,1,0:T(8,128)(2,1)}) custom-call(bf16[32,4096]{1,0:T(8,128)(2,1)} %bitcast.10, bf16[16,4096]{1,0:T(8,128)(2,1)} %bitcast.15, s32[1,128]{1,0:T(1,128)} %refs_2_.1, s32[1,128]{1,0:T(1,128)} %refs_3_.1, f32[1,4096]{1,0:T(1,128)} %refs_4_.1, ...), custom_call_target="tpu_custom_call" | custom-call | flops 17179869184 | bytes 4194304 | tf_op jit(solution)/shard_map/decoder_phases/pallas_call | solution.py:845
  121.4 2.0 %assemble.1 = (bf16[32,4096]{1,0:T(8,128)(2,1)}, bf16[32,4096]{1,0:T(8,128)(2,1)}, f32[16,4096]{1,0:T(8,128)}) custom-call(bf16[4,32,1024]{2,1,0:T(8,128)(2,1)} %get-tuple-element.9.phase, bf16[4,32,1024]{2,1,0:T(8,128)(2,1)} %get-tuple-element.10.stream, bf16[4,16,1024]{2,1,0:T(8,128)(2,1)} %get-tuple-element.11.memory), custom_call_target="tpu_custom_call" | custom-call | tf_op jit(solution)/shard_map/assemble/pallas_call | solution.py:869

commit v4 on v3

--- a/solution.py
+++ b/solution.py
@@ -198,6 +198,9 @@
     def by_distance(i):
         return i + (i // 2) * (5 - 2 * i)
 
+    def far_first(i):
+        return (2 * i) % 3 + 3 * (i // 3)
+
     def near(k):
         return (y + by_distance(k)) % NY
 
@@ -210,7 +213,7 @@
 
     def x_send(step, src_of, dst, sec, lo, at=0):
         def one(k):
-            xp = (x + k) % NX
+            xp = (x + far_first(k)) % NX
             copy(step, src_of(xp), dst, at, dev(sec, xp, y)).start()
 
         each(lo, NX, one)
@@ -371,9 +374,11 @@
 
     def project(step, rows_of, product, stage, landing, own, arrived=None):
         def one(k):
-            yp = near(k)
             if arrived is not None:
+                yp = near(k)
                 arrived(yp)
+            else:
+                yp = (y + far_first(k)) % NY
             stage[yp] = product(rows_of(yp)).astype(BF)
             copy(step, stage.at[yp], landing.at[y], 0, dev(s, x, yp)).start()
 

time: 124 us -> 123 us (level)
  no operation moved by 1% of the time
where the time goes in v4:
time: 123 us
  Pallas kernels  123 us (100%)
    pallas_call x1, Pallas kernels, body(): pl.pallas_call(kernel, out_shape=(jax.ShapeDtypeStruct((NY, ROWS, SL), BF...  121 us

profile of v4, /device:TPU:1, one launch (start us, length us, event | category | flops | bytes accessed | tf_op | source)
XLA Modules:
  0.0 123.2 jit_solution(15156823868867100528)
XLA Ops:
  0.6 120.6 %decoder_phases.1 = (bf16[4,32,1024]{2,1,0:T(8,128)(2,1)}, bf16[4,32,1024]{2,1,0:T(8,128)(2,1)}, bf16[4,16,1024]{2,1,0:T(8,128)(2,1)}) custom-call(bf16[32,4096]{1,0:T(8,128)(2,1)} %bitcast.10, bf16[16,4096]{1,0:T(8,128)(2,1)} %bitcast.15, s32[1,128]{1,0:T(1,128)} %refs_2_.1, s32[1,128]{1,0:T(1,128)} %refs_3_.1, f32[1,4096]{1,0:T(1,128)} %refs_4_.1, ...), custom_call_target="tpu_custom_call" | custom-call | flops 17179869184 | bytes 4194304 | tf_op jit(solution)/shard_map/decoder_phases/pallas_call | solution.py:850
  121.2 2.0 %assemble.1 = (bf16[32,4096]{1,0:T(8,128)(2,1)}, bf16[32,4096]{1,0:T(8,128)(2,1)}, f32[16,4096]{1,0:T(8,128)}) custom-call(bf16[4,32,1024]{2,1,0:T(8,128)(2,1)} %get-tuple-element.9.phase, bf16[4,32,1024]{2,1,0:T(8,128)(2,1)} %get-tuple-element.10.stream, bf16[4,16,1024]{2,1,0:T(8,128)(2,1)} %get-tuple-element.11.memory), custom_call_target="tpu_custom_call" | custom-call | tf_op jit(solution)/shard_map/assemble/pallas_call | solution.py:874
